TPU v7x, 1024 devices: a whole 4x8x16 slice. The times are simulated.
1024 devices in a mesh: blk: 64 (over y_lo, z), grp: 16 (over y_hi, x, core).
Axes of the slice: x: 4, y: 8 (y_hi: 2, y_lo: 4; y = y_hi * 4 + y_lo), z: 16, core: 2. Of those that a mesh axis runs over, the one named last changes fastest.
Arguments:
- embed: bfloat16 [16384, 256], P('blk'), may hold values from -1.5 to 1.5
- state: float32 [16384], P('blk'), may hold values from 0.01 to 1
- relation: float32 [512, 256], replicated, may hold values from -4 to 4
- src_index: int32 [64, 16, 4, 2, 128], P('blk', 'grp'), may hold values from 0 to 255
- dst_index: int32 [64, 16, 4, 2, 128], P('blk', 'grp'), may hold values from 0 to 255
- rel_index: int32 [64, 16, 4, 2, 128], P('blk', 'grp'), may hold values from 0 to 511
- neg_index: int32 [64, 16, 4, 2, 128], P('blk', 'grp'), may hold values from 0 to 255
- counts: int32 [64, 16, 4], P('blk', 'grp'), may hold values from 1 to 2
Outputs:
- new_embed: float32 [16384, 256], P(('blk', 'grp'))
- new_state: float32 [16384], P(('blk', 'grp'))
- dest_grad: float32 [16384, 256], P(('blk', 'grp'))
- rel_grad: float32 [512, 256], replicated
Inputs may be any that keep to these rules, and one draw needn't show every extreme that they name: `counts`: blocks at and after the count are unused.
All inputs are finite; a program needn't handle non-finite values.
Results may differ from a plain program's by a relative error of at most 0.00043.
Values may be sent and summed in bfloat16 or wider, within the bound.
A program may use at most 32 MiB of HBM per device.

v0:
```python
import jax
import jax.numpy as jnp
from jax import lax
from jax.sharding import PartitionSpec as P

STEPS = 4


def shifted(block, axis, distance):
    devices = range(lax.axis_size(axis))
    route = [((i - distance) % len(devices), i) for i in devices]
    return lax.ppermute(block, axis, route)


def bucket(
    source_slab,
    target_slab,
    relation,
    src_rows,
    dst_rows,
    rel_rows,
    neg_rows,
    live_count,
    src_acc,
    dst_acc,
    rel_acc,
):
    features = source_slab.shape[1]
    block_slots = src_rows.shape[0]
    negs_count = neg_rows.shape[1]
    source = source_slab[src_rows]
    target = target_slab[dst_rows]
    negatives = target_slab[neg_rows]
    rel_vals = relation[rel_rows]
    live_mask = (jnp.arange(block_slots, dtype=jnp.int32) < live_count).astype(jnp.float32)
    source_f = source.astype(jnp.float32)
    scaled = source_f * rel_vals
    positive = jnp.sum(scaled * target.astype(jnp.float32), axis=-1)
    scaled_b = scaled.astype(jnp.bfloat16)
    negative = jnp.einsum("bed,bnd->ben", scaled_b, negatives, preferred_element_type=jnp.float32)
    pos_grad = -jax.nn.sigmoid(-positive) * live_mask[:, None]
    neg_grad = (jax.nn.sigmoid(negative) * (live_mask[:, None, None] / negs_count)).astype(
        jnp.bfloat16
    )
    scaled_grad = pos_grad[..., None] * target.astype(jnp.float32)
    scaled_grad = scaled_grad + jnp.einsum(
        "ben,bnd->bed", neg_grad, negatives, preferred_element_type=jnp.float32
    )
    source_g = (scaled_grad * rel_vals).reshape(-1, features)
    rel_g = (scaled_grad * source_f).reshape(-1, features)
    target_g = (pos_grad[..., None] * scaled).reshape(-1, features)
    neg_g = jnp.einsum(
        "ben,bed->bnd", neg_grad, scaled_b, preferred_element_type=jnp.float32
    ).reshape(-1, features)
    src_acc = src_acc.at[src_rows.reshape(-1)].add(source_g)
    dst_acc = dst_acc.at[dst_rows.reshape(-1)].add(target_g)
    dst_acc = dst_acc.at[neg_rows.reshape(-1)].add(neg_g)
    rel_acc = rel_acc.at[rel_rows.reshape(-1)].add(rel_g)
    return (src_acc, dst_acc, rel_acc)


def on_device(embed, state, relation, src_index, dst_index, rel_index, neg_index, counts):
    slab_rows, features = embed.shape
    share_rows = slab_rows // lax.axis_size("grp")
    row_start = lax.axis_index("grp") * share_rows
    target_slab = embed
    src_grad = jnp.zeros((slab_rows, features), jnp.float32)
    rel_grad = jnp.zeros(relation.shape, jnp.float32)
    carried = jnp.zeros((slab_rows, features), jnp.float32)
    for cycle_step in range(STEPS):
        if cycle_step > 0:
            target_slab = shifted(target_slab, "blk", 1)
            carried = shifted(carried, "blk", 1)
        dst_start = carried
        src_grad, dst_part, rel_grad = bucket(
            embed,
            target_slab,
            relation,
            src_index[0, 0, cycle_step],
            dst_index[0, 0, cycle_step],
            rel_index[0, 0, cycle_step],
            neg_index[0, 0, cycle_step],
            counts[0, 0, cycle_step],
            src_grad,
            dst_start,
            rel_grad,
        )
        carried = dst_part
    src_share, carried = (
        lax.psum_scatter(src_grad, "grp", scatter_dimension=0, tiled=True),
        lax.psum_scatter(carried, "grp", scatter_dimension=0, tiled=True),
    )
    rel_total = lax.psum(rel_grad, ("blk", "grp"))
    own_rows = lax.dynamic_slice_in_dim(embed, row_start, share_rows, 0).astype(jnp.float32)
    own_state = lax.dynamic_slice_in_dim(state, row_start, share_rows, 0)
    new_state = own_state + jnp.mean(src_share * src_share, axis=-1)
    new_embed = own_rows - 0.5 * src_share / jnp.sqrt(new_state)[:, None]
    return (new_embed, new_state, carried, rel_total)


def solution(mesh):
    return jax.shard_map(
        on_device,
        mesh=mesh,
        in_specs=(
            P("blk", None),
            P("blk"),
            P(),
            P("blk", "grp", None, None, None),
            P("blk", "grp", None, None, None),
            P("blk", "grp", None, None, None),
            P("blk", "grp", None, None, None),
            P("blk", "grp", None),
        ),
        out_specs=(P(("blk", "grp"), None), P(("blk", "grp")), P(("blk", "grp"), None), P()),
        check_vma=False,
    )
```

profile of v0, /device:TPU:1, one launch (start us, length us, event | category | flops | bytes accessed | tf_op | source)
XLA Modules:
  0.0 618.1 jit_solution(11773012031626854343)
XLA Ops:
  8.1 5.0 collective-permute-start
  17.8 2.0 gather_fusion
  23.9 2.0 scatter_custom_fusion.4
  25.9 2.1 scatter_fusion.3
  28.0 4.0 collective-permute-start.3
  55.1 2.6 scatter_custom_fusion
  57.7 2.2 scatter_custom_fusion.12
  64.0 1.9 gather_fusion.7
  71.6 2.5 scatter_fusion
  74.8 2.2 scatter_fusion.10
  77.0 4.0 collective-permute-start.1
  82.5 2.1 scatter_fusion.4
  85.2 2.1 scatter_fusion.5
  87.3 5.2 collective-permute-start.4
  92.5 4.6 collective-permute-done.1
  101.1 1.8 convert_multiply_fusion.10
  103.5 2.1 scatter_fusion.1
  105.6 2.1 collective-permute-start.2
  108.0 7.2 %collective-permute-done.2 = bf16[256,256]{1,0:T(8,128)(2,1)S(1)} collective-permute-done((bf16[256,256]{1,0:T(8,128)(2,1)S(1)}, bf16[256,256]{1,0:T(8,128)(2,1)S(1)}, u32[]{:S(2)}, u32[]{:S(2)}) %collective-permute-start.2) | collective-permute-done | bytes 131104 | tf_op jit(solution)/shard_map/ppermute | solution.py:12
  119.3 1.8 convert_multiply_fusion.8
  121.8 2.1 scatter_fusion.2
  125.7 2.2 scatter_fusion.11
  128.6 2.2 scatter_fusion.12
  132.4 2.1 scatter_fusion.6
  135.1 2.1 scatter_fusion.7
  137.2 2.1 collective-permute-start.5
  139.6 8.7 %collective-permute-done.5 = f32[256,256]{1,0:T(8,128)S(1)} collective-permute-done((f32[256,256]{1,0:T(8,128)S(1)}, f32[256,256]{1,0:T(8,128)S(1)}, u32[]{:S(2)}, u32[]{:S(2)}) %collective-permute-start.5) | collective-permute-done | bytes 262176 | tf_op jit(solution)/shard_map/ppermute | solution.py:12
  148.4 2.1 scatter_fusion.8
  151.1 2.1 scatter_fusion.9
  153.9 67.1 %reduce-scatter.3.cloned.1.call-done = f32[16,256]{1,0:T(8,128)} async-done(((f32[256,256]{1,0:T(8,128)}), f32[16,256]{1,0:T(8,128)}) %reduce-scatter.3.cloned.1.call-update) | async-done | bytes 16400 | tf_op jit(solution)/shard_map/reduce_scatter | solution.py:90
  223.2 385.6 %all-reduce.2.cloned.1.call-done = f32[512,256]{1,0:T(8,128)} async-done(((f32[512,256]{1,0:T(8,128)}), f32[512,256]{1,0:T(8,128)}) %all-reduce.2.cloned.1.call-update) | async-done | bytes 524304 | tf_op jit(solution)/shard_map/psum | solution.py:93
  608.8 1.9 copy.38
  (184 shorter events, 62.4 us)
Async XLA Ops:
  8.0 14.1 %copy-start = (f32[512,256]{1,0:T(8,128)S(1)}, f32[512,256]{1,0:T(8,128)}, u32[]{:S(2)}) copy-start(f32[512,256]{1,0:T(8,128)} %param.10) | copy-start | bytes 1572868
  8.0 213.0 %reduce-scatter.3.cloned.1.call-start = ((), (), s32[]{:S(2)}) async-start(), calls=%async_computation.2 | async-start | bytes 278528 | tf_op jit(solution)/shard_map/reduce_scatter | solution.py:90
  8.1 53.2 %collective-permute-start = (bf16[256,256]{1,0:T(8,128)(2,1)}, bf16[256,256]{1,0:T(8,128)(2,1)S(1)}, u32[]{:S(2)}, u32[]{:S(2)}) collective-permute-start(bf16[256,256]{1,0:T(8,128)(2,1)} %param.8), channel_id=1, source_target_pairs={{1008,0},{0,16},{16,32},{32,48},{48,64},{64,80},{80,96},{96,112},{... | collective-permute-start | bytes 393224 | tf_op jit(solution)/shard_map/ppermute | solution.py:12
  14.4 1.3 copy-start.18
  15.8 0.7 copy-start.19
  17.8 2.0 copy-start.21
  17.8 2.0 copy-start.1
  28.0 53.8 %collective-permute-start.3 = (f32[256,256]{1,0:T(8,128)S(1)}, f32[256,256]{1,0:T(8,128)S(1)}, u32[]{:S(2)}, u32[]{:S(2)}) collective-permute-start(f32[256,256]{1,0:T(8,128)S(1)} %scatter_fusion.3), channel_id=1, source_target_pairs={{1008,0},{0,16},{16,32},{32,48},{48,64},{64,80},{80,96},{96,112},{... | collective-permute-start | bytes 786440 | tf_op jit(solution)/shard_map/ppermute | solution.py:12
  67.8 1.6 copy-start.5
  67.8 1.6 copy-start.10
  71.6 2.5 copy-start.9
  77.0 20.0 %collective-permute-start.1 = (bf16[256,256]{1,0:T(8,128)(2,1)S(1)}, bf16[256,256]{1,0:T(8,128)(2,1)S(1)}, u32[]{:S(2)}, u32[]{:S(2)}) collective-permute-start(bf16[256,256]{1,0:T(8,128)(2,1)S(1)} %collective-permute-done), channel_id=1, source_target_pairs={{1008,0},{0,16},{16,32},{32,48},{48,64},{64,80},{80,96},{96,112},{... | collective-permute-start | bytes 393224 | tf_op jit(solution)/shard_map/ppermute | solution.py:12
  82.5 2.1 copy-start.6
  87.3 44.4 %collective-permute-start.4 = (f32[256,256]{1,0:T(8,128)S(1)}, f32[256,256]{1,0:T(8,128)S(1)}, u32[]{:S(2)}, u32[]{:S(2)}) collective-permute-start(f32[256,256]{1,0:T(8,128)S(1)} %scatter_fusion.5), channel_id=1, source_target_pairs={{1008,0},{0,16},{16,32},{32,48},{48,64},{64,80},{80,96},{96,112},{... | collective-permute-start | bytes 786440 | tf_op jit(solution)/shard_map/ppermute | solution.py:12
  101.1 1.8 copy-start.15
  103.5 4.2 copy-start.16
  105.6 9.6 %collective-permute-start.2 = (bf16[256,256]{1,0:T(8,128)(2,1)S(1)}, bf16[256,256]{1,0:T(8,128)(2,1)S(1)}, u32[]{:S(2)}, u32[]{:S(2)}) collective-permute-start(bf16[256,256]{1,0:T(8,128)(2,1)S(1)} %collective-permute-done.1), channel_id=1, source_target_pairs={{1008,0},{0,16},{16,32},{32,48},{48,64},{64,80},{80,96},{96,112},{... | collective-permute-start | bytes 393224 | tf_op jit(solution)/shard_map/ppermute | solution.py:12
  119.3 1.8 copy-start.13
  123.9 0.7 copy-start.2
  123.9 0.8 copy-start.36
  124.6 484.2 %all-reduce.2.cloned.1.call-start = ((), (), s32[]{:S(2)}) async-start(), calls=%async_computation.4 | async-start | bytes 1048576 | tf_op jit(solution)/shard_map/psum | solution.py:93
  124.7 1.0 copy-start.7
  124.9 0.8 copy-start.28
  125.7 2.2 copy-start.8
  130.7 0.8 copy-start.3
  131.6 477.3 %reduce-scatter.5.cloned.1.call-start = ((), (), s32[]{:S(2)}) async-start(), calls=%async_computation.3 | async-start | bytes 278528 | tf_op jit(solution)/shard_map/reduce_scatter | solution.py:91
  137.2 2.2 copy-start.14
  137.2 11.2 %collective-permute-start.5 = (f32[256,256]{1,0:T(8,128)S(1)}, f32[256,256]{1,0:T(8,128)S(1)}, u32[]{:S(2)}, u32[]{:S(2)}) collective-permute-start(f32[256,256]{1,0:T(8,128)S(1)} %scatter_fusion.7), channel_id=1, source_target_pairs={{1008,0},{0,16},{16,32},{32,48},{48,64},{64,80},{80,96},{96,112},{... | collective-permute-start | bytes 786440 | tf_op jit(solution)/shard_map/ppermute | solution.py:12
  139.6 8.8 %copy-start.23 = (s32[256,1]{0,1:T(1,128)S(1)}, s32[256,1]{0,1:T(1,128)}, u32[]{:S(2)}) copy-start(s32[256,1]{0,1:T(1,128)} %compare_select_fusion.5) | copy-start | bytes 3076
  153.2 0.7 copy-start.4
  153.9 68.0 %copy-start.39 = (f32[256]{0:T(256)S(1)}, f32[256]{0:T(256)}, u32[]{:S(2)}) copy-start(f32[256]{0:T(256)} %param.9) | copy-start | bytes 3076
  221.0 1.5 copy-start.17
  (20 other events, 13.1 us)
Sparse Core Ops, SparseCore 0:
  124.7 96.2 reduce-scatter.2
  228.3 96.6 reduce-scatter.4
Sparse Core Ops, SparseCore 1:
  131.6 477.1 all-reduce.1
where the time goes:
time: 621 us; the launch traced here: 618 us
  waiting for transfers between devices  473 us (76%)
  other arithmetic  58.5 us (9%)
  local copies, waits for them, and re-layouts  38.8 us (6%)
  starting transfers between devices  22.5 us (4%)
  between operations  16.2 us (3%)
  matrix products  8.84 us (1%)
    psum x1, waiting for transfers between devices, on_device(): rel_total = lax.psum(rel_grad, ('blk', 'grp'))  386 us
    reduce_scatter x1, waiting for transfers between devices, on_device(): lax.psum_scatter(src_grad, 'grp', scatter_dimension=0, tiled=True)  67.1 us
    ppermute x6, starting transfers between devices, shifted(): return lax.ppermute(block, axis, route)  22.4 us
    ppermute x6, waiting for transfers between devices, shifted(): return lax.ppermute(block, axis, route)  20.5 us
    unnamed x87, local copies, waits for them, and re-layouts  17.3 us
  transfers between devices with their start and end apart: 9, of which 5 were waited for; matrix products, arithmetic and copies ran while one was open for 14% of the time, Pallas kernels for 0%

commit v1 on v0

v1 whole, which is shorter than its diff:
```python
import functools

import jax
import jax.numpy as jnp
from jax import lax
from jax.experimental import pallas as pl
from jax.experimental.pallas import tpu as pltpu
from jax.sharding import PartitionSpec as P

NZ = 16
NX = 4
NY = 8
NB = 64
MESH = pl.DeviceIdType.MESH
F32 = jnp.float32
BF16 = jnp.bfloat16


def position():
    b = lax.axis_index("blk")
    g = lax.axis_index("grp")
    z = lax.rem(b, NZ)
    y = lax.div(g, 8) * 4 + lax.div(b, NZ)
    x = lax.rem(lax.div(g, 2), NX)
    c = lax.rem(g, 2)
    return b, g, z, y, x, c


def at(z, y, x, c):
    return (lax.rem(y, 4) * NZ + z, lax.div(y, 4) * 8 + x * 2 + c)


def remote(src, dst, send, recv, where):
    return pltpu.make_async_remote_copy(
        src_ref=src, dst_ref=dst, send_sem=send, recv_sem=recv, device_id=where, device_id_type=MESH
    )


def greet(where):
    pl.semaphore_signal(pltpu.get_barrier_semaphore(), inc=1, device_id=where, device_id_type=MESH)


def exchange_kernel(
    embed, src, dst, rel, neg, counts, slab, index, packed, idx_send, idx_recv, slab_send, slab_recv
):
    b, g, z, y, x, c = position()
    sibling = (b, g + 1 - 2 * c)
    ahead = (lax.rem(b + x, NB), g)
    behind = (lax.rem(b + NB - x, NB), g)
    greet(sibling)
    for d in range(1, NX):
        greet(at(z, y, lax.rem(x + d, NX), c))

    @pl.when(x > 0)
    def _():
        greet(ahead)
        greet(behind)

    for t in range(NX):
        blocks = lax.broadcasted_iota(jnp.int32, (2, 128), 0)
        packed[t, 0:2] = jnp.where(blocks < counts[0, 0, t], src[0, 0, t], -1)
        packed[t, 2:4] = dst[0, 0, t]
        packed[t, 4:6] = rel[0, 0, t]
        packed[t, 6:8] = neg[0, 0, t]
    pl.semaphore_wait(pltpu.get_barrier_semaphore(), jnp.where(x > 0, NX + 2, NX))

    half = pl.ds(pl.multiple_of(c * 128, 128), 128)
    other = pl.ds(pl.multiple_of((1 - c) * 128, 128), 128)

    @pl.when(x > 0)
    def _():
        remote(embed.at[half], slab.at[half], slab_send.at[0], slab_recv.at[0], ahead).start()

    sends = []
    for d in (2, 1, 3):
        there = lax.rem(x + d, NX)
        copy = remote(
            packed.at[there], index.at[x], idx_send.at[d - 1], idx_recv.at[d - 1], at(z, y, there, c)
        )
        copy.start()
        sends.append(copy)
    index[pl.ds(x, 1)] = packed[pl.ds(x, 1)]

    @pl.when(x == 0)
    def _():
        slab[...] = embed[...]

    @pl.when(x > 0)
    def _():
        first = remote(embed.at[half], slab.at[half], slab_send.at[0], slab_recv.at[0], ahead)
        second = remote(slab.at[half], slab.at[half], slab_send.at[1], slab_recv.at[1], sibling)
        first.wait_recv()
        second.start()
        first.wait_send()
        second.wait_send()
        remote(slab.at[other], slab.at[other], slab_send.at[1], slab_recv.at[1], sibling).wait_recv()

    for copy in sends:
        copy.wait()


def compute_kernel(
    index, source, slab, relation, src_out, dst_out, rel_out, parts, hot_src, hot_dst, hot_rel, g_src, g_dst, g_rel
):
    r = relation[...]
    high = r.astype(BF16)
    rest = r - high.astype(F32)
    mid = rest.astype(BF16)
    parts[:, 0:256] = high
    parts[:, 256:512] = mid
    parts[:, 512:768] = (rest - mid.astype(F32)).astype(BF16)

    def hot(hit):
        return jnp.where(hit, 1.0, 0.0).astype(BF16)

    def split(ref, rows, value):
        top = value.astype(BF16)
        ref[rows, 0:256] = top
        ref[rows, 256:512] = (value - top.astype(F32)).astype(BF16)

    def dot(a, b):
        return jnp.dot(a, b, preferred_element_type=F32)

    lane = lax.broadcasted_iota(jnp.int32, (256, 256), 1)
    lane_r = lax.broadcasted_iota(jnp.int32, (256, 512), 1)
    sub = lax.broadcasted_iota(jnp.int32, (256, 256), 0)
    sub_r = lax.broadcasted_iota(jnp.int32, (512, 256), 0)
    for k in range(NX):
        rows = index[k]
        columns = rows.T

        def row(i):
            return jnp.concatenate([rows[2 * i : 2 * i + 1], rows[2 * i + 1 : 2 * i + 2]], axis=1)

        def column(i):
            return jnp.concatenate([columns[:, 2 * i : 2 * i + 1], columns[:, 2 * i + 1 : 2 * i + 2]], axis=0)

        edges = slice(k * 256, k * 256 + 256)
        negs = slice(1024 + k * 256, 1024 + k * 256 + 256)
        hot_src[:, edges] = hot(sub == row(0))
        hot_dst[:, edges] = hot(sub == row(1))
        hot_dst[:, negs] = hot(sub == row(3))
        hot_rel[:, edges] = hot(sub_r == row(2))
        src_v = dot(hot(lane == column(0)), source[...])
        dst_v = dot(hot(lane == column(1)), slab[...])
        neg_v = dot(hot(lane == column(3)), slab[...]).astype(BF16)
        pieces = dot(hot(lane_r == column(2)), parts[...])
        rel_v = (pieces[:, 0:256] + pieces[:, 256:512]) + pieces[:, 512:768]
        scaled = src_v * rel_v
        positive = jnp.sum(scaled * dst_v, axis=1, keepdims=True)
        pos_grad = -jax.nn.sigmoid(-positive)
        scaled_b = scaled.astype(BF16)
        from_neg = []
        neg_g = []
        for j in range(2):
            block = slice(j * 128, j * 128 + 128)
            s, n = scaled_b[block], neg_v[block]
            score = lax.dot_general(s, n, (((1,), (1,)), ((), ())), preferred_element_type=F32)
            weight = (jax.nn.sigmoid(score) * (1.0 / 128.0)).astype(BF16)
            from_neg.append(dot(weight, n))
            neg_g.append(lax.dot_general(weight, s, (((0,), (0,)), ((), ())), preferred_element_type=F32))
        scaled_grad = pos_grad * dst_v + jnp.concatenate(from_neg, axis=0)
        split(g_rel, edges, scaled_grad * src_v)
        split(g_src, edges, scaled_grad * rel_v)
        split(g_dst, edges, pos_grad * scaled)
        split(g_dst, negs, jnp.concatenate(neg_g, axis=0))

    def total(h, g):
        both = dot(h[...], g[...])
        return both[:, 0:256] + both[:, 256:512]

    rel_out[...] = total(hot_rel, g_rel).reshape(rel_out.shape)
    src_out[...] = total(hot_src, g_src).reshape(src_out.shape)
    dst_out[...] = total(hot_dst, g_dst).reshape(dst_out.shape)


def reduce_kernel(
    rel_in,
    src_in,
    dst_in,
    embed,
    state,
    new_embed,
    new_state,
    dest_out,
    rel_out,
    rel_pair,
    src_pair,
    dst_pair,
    rel_xy,
    rel_z,
    src_x,
    dst_x,
    src_half,
    src_y,
    dst_y,
    send,
    recv,
    dst_send,
    dst_recv,
):
    b, g, z, y, x, c = position()
    sibling = (b, g + 1 - 2 * c)
    opposite = at(z, lax.rem(y + 4, NY), x, c)
    yh = lax.div(y, 4)
    base = lax.rem(b + 3 + NB - x, NB)
    row_of = lax.div(g, 8) * 8 + c
    mine = x * NY + y

    offsets = [(dx, dy) for dx in (2, 1, 3, 0) for dy in (4, 3, 5, 2, 6, 1, 7, 0) if (dx, dy) != (0, 0)]
    z_offsets = (8, 7, 9, 6, 10, 5, 11, 4, 12, 3, 13, 2, 14, 1, 15)

    def plane(dx, dy):
        px, py = lax.rem(x + dx, NX), lax.rem(y + dy, NY)
        return px * NY + py, at(z, py, px, c)

    greet(sibling)
    for dz in z_offsets:
        greet(at(lax.rem(z + dz, NZ), y, x, c))
    for dx, dy in offsets:
        greet(plane(dx, dy)[1])
    for t in range(NX):
        to = (base, row_of + 2 * t)
        source = (lax.rem(b + NB - 3 + t, NB), row_of + 2 * t)

        @pl.when(jnp.logical_or(x != 3, t != 3))
        def _():
            greet(to)
            greet(source)

    pl.semaphore_wait(pltpu.get_barrier_semaphore(), 1 + 15 + 31 + jnp.where(x == 3, 6, 8))

    def pair(source, target, i):
        return remote(source, target, send.at[i], recv.at[i], sibling)

    rel_c = pair(rel_in.at[1 - c], rel_pair, 0)
    src_c = pair(src_in.at[:, :, 1 - c], src_pair, 1)
    dst_c = pair(dst_in.at[:, :, 1 - c], dst_pair, 2)
    rel_c.start()
    src_c.start()
    dst_c.start()

    rel_c.wait()
    rel_pair[...] = rel_pair[...] + rel_in[pl.ds(c, 1)][0]
    for i, (dx, dy) in enumerate(offsets):
        chunk, where = plane(dx, dy)
        remote(rel_pair.at[chunk], rel_xy.at[i], send.at[3], recv.at[3], where).start()

    src_c.wait()
    src_pair[...] = src_pair[...] + src_in[:, :, pl.ds(c, 1)].reshape(2, 4, 16, 256)
    src_sends = []
    for d in (2, 1, 3):
        px = lax.rem(x + d, NX)
        copy = remote(src_pair.at[:, px], src_x.at[d], send.at[4 + d], recv.at[4 + d], at(z, y, px, c))
        copy.start()
        src_sends.append(copy)
    dst_c.wait()
    dst_pair[...] = dst_pair[...] + dst_in[:, :, pl.ds(c, 1)].reshape(2, 4, 16, 256)
    for t in range(NX):
        to = (base, row_of + 2 * t)

        @pl.when(jnp.logical_or(x != 3, t != 3))
        def _():
            remote(dst_pair.at[:, t], dst_x.at[x], dst_send.at[t], dst_recv.at[x], to).start()

    @pl.when(x == 3)
    def _():
        dst_x[3] = dst_pair[:, 3]

    def chunks(ref, n, sem):
        return pltpu.make_async_copy(ref.at[pl.ds(0, n)], ref.at[pl.ds(0, n)], sem)

    chunks(rel_xy, 31, recv.at[3]).wait()
    own = rel_pair[pl.ds(mine, 1)][0] + jnp.sum(rel_xy[...], axis=0)
    rel_z[pl.ds(z, 1)] = own[None]
    for dz in z_offsets:
        where = at(lax.rem(z + dz, NZ), y, x, c)
        remote(rel_z.at[z], rel_z.at[z], send.at[8], recv.at[8], where).start()

    for copy in src_sends:
        copy.wait_recv()
    src_half[...] = (src_pair[:, pl.ds(x, 1)].reshape(2, 16, 256) + src_x[1]) + (src_x[2] + src_x[3])
    src_far = remote(src_half.at[1 - yh], src_y, send.at[9], recv.at[9], opposite)
    src_far.start()
    for t in range(NX):
        source = (lax.rem(b + NB - 3 + t, NB), row_of + 2 * t)

        @pl.when(jnp.logical_or(x != 3, t != 3))
        def _():
            remote(dst_pair.at[:, t], dst_x.at[t], dst_send.at[t], dst_recv.at[t], source).wait_recv()

    dst_x[0] = (dst_x[0] + dst_x[1]) + (dst_x[2] + dst_x[3])
    dst_far = remote(dst_x.at[0, 1 - yh], dst_y, send.at[10], recv.at[10], opposite)
    dst_far.start()

    src_far.wait_recv()
    total = src_half[pl.ds(yh, 1)][0] + src_y[...]
    lane = lax.broadcasted_iota(jnp.int32, (16, 256), 1)
    line = lax.broadcasted_iota(jnp.int32, (16, 256), 0)
    old = jnp.sum(jnp.where(lane == line + g * 16, state[...], 0.0), axis=1, keepdims=True)
    fresh = old + jnp.sum(total * total, axis=1, keepdims=True) * (1.0 / 256.0)
    own_rows = embed[pl.ds(pl.multiple_of(g * 16, 16), 16)].astype(F32)
    new_embed[...] = own_rows - 0.5 * total / jnp.sqrt(fresh)
    lane16 = lax.broadcasted_iota(jnp.int32, (16, 16), 1)
    line16 = lax.broadcasted_iota(jnp.int32, (16, 16), 0)
    new_state[...] = jnp.sum(jnp.where(lane16 == line16, fresh, 0.0), axis=0, keepdims=True)
    dst_far.wait_recv()
    dest_out[...] = dst_x[0, pl.ds(yh, 1)].reshape(16, 256) + dst_y[...]

    chunks(rel_z, 15, recv.at[8]).wait()
    rel_out[pl.ds(c, 1), pl.ds(mine, 1)] = jnp.sum(rel_z[...], axis=0)[None, None]
    for dx, dy in offsets:
        _, where = plane(dx, dy)
        remote(rel_out.at[c, mine], rel_out.at[c, mine], send.at[11], recv.at[11], where).start()
    chunks(rel_xy, 31, recv.at[11]).wait()
    last = remote(rel_out.at[c], rel_out.at[c], send.at[12], recv.at[12], sibling)
    last.start()
    chunks(rel_xy, 31, send.at[3]).wait()
    chunks(rel_z, 15, send.at[8]).wait()
    chunks(rel_xy, 31, send.at[11]).wait()
    for copy in src_sends:
        copy.wait_send()
    for t in range(NX):

        @pl.when(jnp.logical_or(x != 3, t != 3))
        def _():
            remote(dst_pair.at[:, t], dst_x.at[x], dst_send.at[t], dst_recv.at[x], sibling).wait_send()

    src_far.wait_send()
    dst_far.wait_send()
    last.wait_send()
    remote(rel_out.at[1 - c], rel_out.at[1 - c], send.at[12], recv.at[12], sibling).wait_recv()


def on_device(embed, state, relation, src_index, dst_index, rel_index, neg_index, counts):
    vmem = pl.BlockSpec(memory_space=pltpu.VMEM)
    smem = pl.BlockSpec(memory_space=pltpu.SMEM)
    dma = pltpu.SemaphoreType.DMA

    def params(**more):
        return pltpu.CompilerParams(vmem_limit_bytes=48 << 20, **more)

    slab, index = pl.pallas_call(
        exchange_kernel,
        out_shape=[jax.ShapeDtypeStruct((256, 256), BF16), jax.ShapeDtypeStruct((4, 8, 128), jnp.int32)],
        in_specs=[vmem] * 5 + [smem],
        out_specs=[vmem] * 2,
        scratch_shapes=[pltpu.VMEM((4, 8, 128), jnp.int32), dma((3,)), dma((3,)), dma((2,)), dma((2,))],
        compiler_params=params(collective_id=0, has_side_effects=True),
        name="exchange",
    )(embed, src_index, dst_index, rel_index, neg_index, counts)
    src_sum, dst_sum, rel_sum = pl.pallas_call(
        compute_kernel,
        out_shape=[
            jax.ShapeDtypeStruct((2, 4, 2, 16, 256), F32),
            jax.ShapeDtypeStruct((2, 4, 2, 16, 256), F32),
            jax.ShapeDtypeStruct((2, 32, 8, 256), F32),
        ],
        in_specs=[vmem] * 4,
        out_specs=[vmem] * 3,
        scratch_shapes=[
            pltpu.VMEM((512, 768), BF16),
            pltpu.VMEM((256, 1024), BF16),
            pltpu.VMEM((256, 2048), BF16),
            pltpu.VMEM((512, 1024), BF16),
            pltpu.VMEM((1024, 512), BF16),
            pltpu.VMEM((2048, 512), BF16),
            pltpu.VMEM((1024, 512), BF16),
        ],
        compiler_params=params(),
        name="buckets",
    )(index, embed, slab, relation)
    new_embed, new_state, dest, rel_grad = pl.pallas_call(
        reduce_kernel,
        out_shape=[
            jax.ShapeDtypeStruct((16, 256), F32),
            jax.ShapeDtypeStruct((1, 16), F32),
            jax.ShapeDtypeStruct((16, 256), F32),
            jax.ShapeDtypeStruct((2, 32, 8, 256), F32),
        ],
        in_specs=[vmem] * 5,
        out_specs=[vmem] * 4,
        scratch_shapes=[
            pltpu.VMEM((32, 8, 256), F32),
            pltpu.VMEM((2, 4, 16, 256), F32),
            pltpu.VMEM((2, 4, 16, 256), F32),
            pltpu.VMEM((31, 8, 256), F32),
            pltpu.VMEM((16, 8, 256), F32),
            pltpu.VMEM((4, 2, 16, 256), F32),
            pltpu.VMEM((4, 2, 16, 256), F32),
            pltpu.VMEM((2, 16, 256), F32),
            pltpu.VMEM((16, 256), F32),
            pltpu.VMEM((16, 256), F32),
            dma((13,)),
            dma((13,)),
            dma((4,)),
            dma((4,)),
        ],
        compiler_params=params(collective_id=1, has_side_effects=True),
        name="reduce",
    )(rel_sum, src_sum, dst_sum, embed, state.reshape(1, 256))
    return (new_embed, new_state.reshape(16), dest, rel_grad.reshape(512, 256))


def solution(mesh):
    return jax.shard_map(
        on_device,
        mesh=mesh,
        in_specs=(
            P("blk", None),
            P("blk"),
            P(),
            P("blk", "grp", None, None, None),
            P("blk", "grp", None, None, None),
            P("blk", "grp", None, None, None),
            P("blk", "grp", None, None, None),
            P("blk", "grp", None),
        ),
        out_specs=(P(("blk", "grp"), None), P(("blk", "grp")), P(("blk", "grp"), None), P()),
        check_vma=False,
    )
```

time: 621 us -> 81.1 us (0.13)
  waiting for transfers between devices: 473 us -> 0 us
  Pallas kernels: 0 us -> 71.5 us
  other arithmetic: 58.5 us -> 0 us
  local copies, waits for them, and re-layouts: 38.8 us -> 8.52 us
  starting transfers between devices: 22.5 us -> 0 us
  between operations: 16.2 us -> 0.69 us
  matrix products: 8.84 us -> 0 us
    psum x1 -> x0, waiting for transfers between devices: 386 us -> none  [on_device(): rel_total = lax.psum(rel_grad, ('blk', 'grp'))]
    pallas_call x0 -> x3, Pallas kernels: none -> 71.5 us  [the longest x1 41.1 us: on_device(): pl.pallas_call(reduce_kernel, out_shape=[jax.ShapeDtypeStruct((16, 256),...]
    reduce_scatter x2 -> x0, waiting for transfers between devices: 67.1 us -> none  [the longest x1 67.1 us: on_device(): lax.psum_scatter(src_grad, 'grp', scatter_dimension=0, tiled=True)]
    scatter-add x16 -> x0, other arithmetic: 34.5 us -> none  [the longest x4 9.25 us: bucket(): src_acc = src_acc.at[src_rows.reshape(-1)].add(source_g)]
    ppermute x6 -> x0, starting transfers between devices: 22.4 us -> none  [shifted(): return lax.ppermute(block, axis, route)]
    ppermute x6 -> x0, waiting for transfers between devices: 20.5 us -> none  [shifted(): return lax.ppermute(block, axis, route)]
    gather x16 -> x0, local copies, waits for them, and re-layouts: 20.1 us -> none  [the longest x4 5.54 us: bucket(): negatives = target_slab[neg_rows]]
    dot_general x12 -> x0, matrix products: 8.84 us -> none  [the longest x4 5.53 us: bucket(): jnp.einsum('ben,bnd->bed', neg_grad, negatives, preferred_element_type=jn...]
  transfers between devices with their start and end apart: 9 -> 0, of which waited for: 5 -> 0; matrix products, arithmetic and copies ran while one was open for 14% -> 0% of each run, Pallas kernels for 0% -> 0%
where the time goes in v1:
time: 81.1 us; the launch traced here: 80.7 us
  Pallas kernels  71.5 us (88%)
  local copies, waits for them, and re-layouts  8.52 us (11%)
    pallas_call x1, Pallas kernels, on_device(): pl.pallas_call(reduce_kernel, out_shape=[jax.ShapeDtypeStruct((16, 256),...  41.1 us
    pallas_call x1, Pallas kernels, on_device(): pl.pallas_call(exchange_kernel, out_shape=[jax.ShapeDtypeStruct((256, 256...  25.1 us
    unnamed x20, local copies, waits for them, and re-layouts  8.52 us
    pallas_call x1, Pallas kernels, on_device(): pl.pallas_call(compute_kernel, out_shape=[jax.ShapeDtypeStruct((2, 4, 2,...  5.35 us

profile of v1, /device:TPU:1, one launch (start us, length us, event | category | flops | bytes accessed | tf_op | source)
XLA Modules:
  0.0 80.7 jit_solution(8012818129922992465)
XLA Ops:
  0.6 0.0 copy-start.7
  0.6 0.6 copy-done.7
  1.3 0.0 copy-start
  1.3 0.9 %copy-done = bf16[256,256]{1,0:T(8,128)(2,1)S(1)} copy-done((bf16[256,256]{1,0:T(8,128)(2,1)S(1)}, bf16[256,256]{1,0:T(8,128)(2,1)}, u32[]{:S(2)}) %copy-start) | copy-done | bytes 131096
  2.2 0.0 copy-start.2
  2.2 0.7 copy-done.2
  2.9 0.0 copy-start.3
  2.9 0.7 copy-done.3
  3.6 0.0 copy-start.4
  3.6 0.7 copy-done.4
  4.3 0.0 copy-start.5
  4.3 0.7 copy-done.5
  4.9 25.1 %exchange.1 = (bf16[256,256]{1,0:T(8,128)(2,1)S(1)}, s32[4,8,128]{2,1,0:T(8,128)S(1)}) custom-call(bf16[256,256]{1,0:T(8,128)(2,1)S(1)} %copy-done, s32[1,1,4,2,128]{4,3,2,1,0:T(2,128)S(1)} %copy-done.2, s32[1,1,4,2,128]{4,3,2,1,0:T(2,128)S(1)} %copy-done.3, s32[1,1,4,2,128]{4,3,2,1,0:T(2,128)S(1)} %copy-done.4, s32[1,1,4,2,128]{4,3,2,1,0:T(2,128)S(1)} %copy-done.5, ...), custom_call_target="tpu_custom_call" | custom-call | tf_op jit(solution)/shard_map/exchange/pallas_call | solution.py:343
  30.0 0.0 copy-start.1
  30.0 1.0 %copy-done.1 = f32[512,256]{1,0:T(8,128)S(1)} copy-done((f32[512,256]{1,0:T(8,128)S(1)}, f32[512,256]{1,0:T(8,128)}, u32[]{:S(2)}) %copy-start.1) | copy-done | bytes 524312
  31.1 5.4 %buckets.1 = (f32[2,4,2,16,256]{4,3,2,1,0:T(8,128)S(1)}, f32[2,4,2,16,256]{4,3,2,1,0:T(8,128)S(1)}, f32[2,32,8,256]{3,2,1,0:T(8,128)S(1)}) custom-call(s32[4,8,128]{2,1,0:T(8,128)S(1)} %get-tuple-element.13.index, bf16[256,256]{1,0:T(8,128)(2,1)S(1)} %copy-done, bf16[256,256]{1,0:T(8,128)(2,1)S(1)} %get-tuple-element.14.slab, f32[512,256]{1,0:T(8,128)S(1)} %copy-done.1), custom_call_target="tpu_custom_call" | custom-call | tf_op jit(solution)/shard_map/buckets/pallas_call | solution.py:352
  36.4 0.0 copy-start.6
  36.4 0.7 copy-done.6
  37.1 41.1 %reduce.1 = (f32[16,256]{1,0:T(8,128)S(1)}, f32[1,16]{1,0:T(1,128)S(1)}, f32[16,256]{1,0:T(8,128)S(1)}, f32[2,32,8,256]{3,2,1,0:T(8,128)S(1)}) custom-call(f32[2,32,8,256]{3,2,1,0:T(8,128)S(1)} %get-tuple-element.15.rel_in, f32[2,4,2,16,256]{4,3,2,1,0:T(8,128)S(1)} %get-tuple-element.16.src_in, f32[2,4,2,16,256]{4,3,2,1,0:T(8,128)S(1)} %get-tuple-element.17.dst_in, ...), custom_call_target="tpu_custom_call" | custom-call | tf_op jit(solution)/shard_map/reduce/pallas_call | solution.py:373
  78.2 0.6 copy.16
  78.8 0.5 copy.17
  79.3 0.6 copy.18
  79.9 0.8 copy.19
Async XLA Ops:
  0.6 0.7 copy-start.7
  1.3 0.9 %copy-start = (bf16[256,256]{1,0:T(8,128)(2,1)S(1)}, bf16[256,256]{1,0:T(8,128)(2,1)}, u32[]{:S(2)}) copy-start(bf16[256,256]{1,0:T(8,128)(2,1)} %embed.3) | copy-start | bytes 393220
  2.2 0.7 copy-start.2
  2.9 0.7 copy-start.3
  3.6 0.7 copy-start.4
  4.3 0.7 copy-start.5
  30.0 1.0 %copy-start.1 = (f32[512,256]{1,0:T(8,128)S(1)}, f32[512,256]{1,0:T(8,128)}, u32[]{:S(2)}) copy-start(f32[512,256]{1,0:T(8,128)} %relation.1) | copy-start | bytes 1572868
  36.4 0.7 copy-start.6

commit v2 on v1

v2 whole, which is shorter than its diff:
```python
import jax
import jax.numpy as jnp
from jax import lax
from jax.experimental import pallas as pl
from jax.experimental.pallas import tpu as pltpu
from jax.sharding import PartitionSpec as P

NZ = 16
NX = 4
NY = 8
NB = 64
MESH = pl.DeviceIdType.MESH
F32 = jnp.float32
BF16 = jnp.bfloat16


def position():
    b = lax.axis_index("blk")
    g = lax.axis_index("grp")
    z = lax.rem(b, NZ)
    y = lax.div(g, 8) * 4 + lax.div(b, NZ)
    x = lax.rem(lax.div(g, 2), NX)
    c = lax.rem(g, 2)
    return b, g, z, y, x, c


def at(z, y, x, c):
    return (lax.rem(y, 4) * NZ + z, lax.div(y, 4) * 8 + x * 2 + c)


def remote(src, dst, send, recv, where):
    return pltpu.make_async_remote_copy(
        src_ref=src, dst_ref=dst, send_sem=send, recv_sem=recv, device_id=where, device_id_type=MESH
    )


def greet(where):
    pl.semaphore_signal(pltpu.get_barrier_semaphore(), inc=1, device_id=where, device_id_type=MESH)


def dot(a, b):
    return jnp.dot(a, b, preferred_element_type=F32)


def hot(hit):
    return jnp.where(hit, 1.0, 0.0).astype(BF16)


def columns_of(rows):
    turned = rows.T
    return jnp.concatenate([turned[:, 0:1], turned[:, 1:2]], axis=0)


def line_of(rows):
    return jnp.concatenate([rows[0:1], rows[1:2]], axis=1)


def exchange_kernel(
    embed,
    relation,
    src,
    dst,
    rel,
    neg,
    counts,
    slab,
    index,
    src_rows,
    rel_rows,
    hot_src,
    hot_dst,
    hot_rel,
    own,
    table,
    parts,
    loaded,
    live,
    packed,
    load_sem,
    idx_send,
    idx_recv,
    slab_send,
    slab_recv,
):
    b, g, z, y, x, c = position()
    loads = [pltpu.make_async_copy(ref.at[0, 0], loaded.at[i], load_sem.at[i]) for i, ref in enumerate((src, dst, rel, neg))]
    loads.append(pltpu.make_async_copy(counts.at[0], live, load_sem.at[4]))
    load_own = pltpu.make_async_copy(embed, own, load_sem.at[5])
    load_table = pltpu.make_async_copy(relation, table, load_sem.at[6])
    for copy in loads:
        copy.start()
    load_own.start()
    load_table.start()
    sibling = (b, g + 1 - 2 * c)
    ahead = (lax.rem(b + x, NB), g)
    behind = (lax.rem(b + NB - x, NB), g)
    greet(sibling)
    for d in range(1, NX):
        greet(at(z, y, lax.rem(x + d, NX), c))

    @pl.when(x > 0)
    def _():
        greet(ahead)
        greet(behind)

    for copy in loads:
        copy.wait()
    blocks = lax.broadcasted_iota(jnp.int32, (2, 128), 0)
    spots = lax.broadcasted_iota(jnp.int32, (1, 4), 1)
    for t in range(NX):
        count = jnp.sum(jnp.where(spots == t, live[...], 0), axis=1, keepdims=True)
        packed[t, 0] = jnp.where(blocks < count, loaded[0, t], -1)
        for i in range(1, 4):
            packed[t, i] = loaded[i, t]
    load_own.wait()
    pl.semaphore_wait(pltpu.get_barrier_semaphore(), jnp.where(x > 0, NX + 2, NX))

    half = pl.ds(pl.multiple_of(c * 128, 128), 128)
    other = pl.ds(pl.multiple_of((1 - c) * 128, 128), 128)

    sends = []
    for d in (2, 1, 3):
        there = lax.rem(x + d, NX)
        copy = remote(packed.at[there], index.at[x], idx_send.at[d - 1], idx_recv.at[d - 1], at(z, y, there, c))
        copy.start()
        sends.append(copy)

    @pl.when(x > 0)
    def _():
        remote(own.at[half], slab.at[half], slab_send.at[0], slab_recv.at[0], ahead).start()

    index[pl.ds(x, 1)] = packed[pl.ds(x, 1)]

    @pl.when(x == 0)
    def _():
        slab[...] = own[...]

    load_table.wait()
    r = table[...]
    high = r.astype(BF16)
    rest = r - high.astype(F32)
    middle = rest.astype(BF16)
    parts[:, 0:256] = high
    parts[:, 256:512] = middle
    parts[:, 512:768] = (rest - middle.astype(F32)).astype(BF16)
    for copy in sends:
        copy.wait()

    lane = lax.broadcasted_iota(jnp.int32, (256, 256), 1)
    lane_r = lax.broadcasted_iota(jnp.int32, (256, 512), 1)
    sub = lax.broadcasted_iota(jnp.int32, (256, 256), 0)
    sub_r = lax.broadcasted_iota(jnp.int32, (2, 256, 256), 0) * 256 + lax.broadcasted_iota(jnp.int32, (2, 256, 256), 1)
    for k in range(NX):
        edges = slice(k * 256, k * 256 + 256)
        negs = slice(1024 + k * 256, 1024 + k * 256 + 256)
        src_rows[edges] = dot(hot(lane == columns_of(index[k, 0])), own[...])
        pieces = dot(hot(lane_r == columns_of(index[k, 2])), parts[...])
        rel_rows[edges] = (pieces[:, 0:256] + pieces[:, 256:512]) + pieces[:, 512:768]
        hot_src[:, edges] = hot(sub == line_of(index[k, 0]))
        hot_dst[:, edges] = hot(sub == line_of(index[k, 1]))
        hot_dst[:, negs] = hot(sub == line_of(index[k, 3]))
        hot_rel[:, :, edges] = hot(sub_r == line_of(index[k, 2])[None])

    @pl.when(x > 0)
    def _():
        first = remote(own.at[half], slab.at[half], slab_send.at[0], slab_recv.at[0], ahead)
        second = remote(slab.at[half], slab.at[half], slab_send.at[1], slab_recv.at[1], sibling)
        first.wait_recv()
        second.start()
        first.wait_send()
        second.wait_send()
        remote(slab.at[other], slab.at[other], slab_send.at[1], slab_recv.at[1], sibling).wait_recv()


def bucket_gradients(index, slab, src_rows, rel_rows, g_src, g_dst, g_rel):
    def split(ref, rows, value):
        top = value.astype(BF16)
        ref[rows, 0:256] = top
        ref[rows, 256:512] = (value - top.astype(F32)).astype(BF16)

    lane = lax.broadcasted_iota(jnp.int32, (256, 256), 1)
    for k in range(NX):
        edges = slice(k * 256, k * 256 + 256)
        negs = slice(1024 + k * 256, 1024 + k * 256 + 256)
        src_v = src_rows[edges]
        rel_v = rel_rows[edges]
        dst_v = dot(hot(lane == columns_of(index[k, 1])), slab[...])
        neg_v = dot(hot(lane == columns_of(index[k, 3])), slab[...]).astype(BF16)
        scaled = src_v * rel_v
        positive = jnp.sum(scaled * dst_v, axis=1, keepdims=True)
        pos_grad = -jax.nn.sigmoid(-positive)
        scaled_b = scaled.astype(BF16)
        from_neg = []
        neg_g = []
        for j in range(2):
            block = slice(j * 128, j * 128 + 128)
            s, n = scaled_b[block], neg_v[block]
            score = lax.dot_general(s, n, (((1,), (1,)), ((), ())), preferred_element_type=F32)
            weight = (jax.nn.sigmoid(score) * (1.0 / 128.0)).astype(BF16)
            from_neg.append(dot(weight, n))
            neg_g.append(lax.dot_general(weight, s, (((0,), (0,)), ((), ())), preferred_element_type=F32))
        scaled_grad = pos_grad * dst_v + jnp.concatenate(from_neg, axis=0)
        split(g_rel, edges, scaled_grad * src_v)
        split(g_src, edges, scaled_grad * rel_v)
        split(g_dst, edges, pos_grad * scaled)
        split(g_dst, negs, jnp.concatenate(neg_g, axis=0))


def both_terms(h, g):
    both = dot(h, g)
    return both[:, 0:256] + both[:, 256:512]


def reduce_kernel(
    slab,
    index,
    src_rows,
    rel_rows,
    hot_src,
    hot_dst,
    hot_rel,
    embed,
    state,
    new_embed,
    new_state,
    dest_out,
    rel_out,
    g_src,
    g_dst,
    g_rel,
    own_rows,
    own_state,
    rel_far,
    rel_near,
    src_part,
    dst_part,
    rel_pair,
    src_pair,
    dst_pair,
    rel_xy,
    rel_z,
    src_x,
    dst_x,
    src_half,
    src_y,
    dst_y,
    send,
    recv,
    dst_send,
    dst_recv,
    all_recv,
    load_sem,
):
    b, g, z, y, x, c = position()
    sibling = (b, g + 1 - 2 * c)
    opposite = at(z, lax.rem(y + 4, NY), x, c)
    yh = lax.div(y, 4)
    base = lax.rem(b + 3 + NB - x, NB)
    row_of = lax.div(g, 8) * 8 + c
    mine = x * NY + y

    y_order = (4, 3, 5, 2, 6, 1, 7, 0)
    offsets = [(dx, dy) for dx in (2, 1, 3, 0) for dy in y_order if (dx, dy) != (0, 0)]
    z_offsets = (8, 7, 9, 6, 10, 5, 11, 4, 12, 3, 13, 2, 14, 1, 15)

    def plane(dx, dy):
        px, py = lax.rem(x + dx, NX), lax.rem(y + dy, NY)
        return px * NY + py, at(z, py, px, c)

    for dz in z_offsets:
        greet(at(lax.rem(z + dz, NZ), y, x, c))
    for dx, dy in offsets:
        greet(plane(dx, dy)[1])
    for t in range(NX):
        to = (base, row_of + 2 * t)
        source = (lax.rem(b + NB - 3 + t, NB), row_of + 2 * t)

        @pl.when(jnp.logical_or(x != 3, t != 3))
        def _():
            greet(to)
            greet(source)

    greet(sibling)
    load_rows = pltpu.make_async_copy(embed.at[pl.ds(pl.multiple_of(g * 16, 16), 16)], own_rows, load_sem.at[0])
    load_state = pltpu.make_async_copy(state, own_state, load_sem.at[1])
    load_rows.start()
    load_state.start()

    bucket_gradients(index, slab, src_rows, rel_rows, g_src, g_dst, g_rel)
    rel_far[...] = both_terms(hot_rel[pl.ds(1 - c, 1)][0], g_rel[...]).reshape(32, 8, 256)
    pl.semaphore_wait(pltpu.get_barrier_semaphore(), 1 + 15 + 31 + jnp.where(x == 3, 6, 8))

    def pair(source, target, i):
        return remote(source, target, send.at[i], recv.at[i], sibling)

    rel_c = pair(rel_far, rel_pair, 0)
    src_c = pair(src_part.at[:, :, 1 - c], src_pair, 1)
    dst_c = pair(dst_part.at[:, :, 1 - c], dst_pair, 2)
    rel_c.start()
    rel_near[...] = both_terms(hot_rel[pl.ds(c, 1)][0], g_rel[...]).reshape(32, 8, 256)

    rel_c.wait_recv()
    rel_near[...] = rel_near[...] + rel_pair[...]
    for i, (dx, dy) in enumerate(offsets):
        chunk, where = plane(dx, dy)
        remote(rel_near.at[chunk], rel_xy.at[i], send.at[3], recv.at[3], where).start()

    src_part[...] = both_terms(hot_src[...], g_src[...]).reshape(2, 4, 2, 16, 256)
    src_c.start()
    dst_part[...] = both_terms(hot_dst[...], g_dst[...]).reshape(2, 4, 2, 16, 256)
    dst_c.start()
    src_c.wait_recv()
    src_pair[...] = src_pair[...] + src_part[:, :, pl.ds(c, 1)].reshape(2, 4, 16, 256)
    src_sends = []
    for d in (2, 1, 3):
        px = lax.rem(x + d, NX)
        copy = remote(src_pair.at[:, px], src_x.at[d], send.at[4 + d], recv.at[4 + d], at(z, y, px, c))
        copy.start()
        src_sends.append(copy)
    dst_c.wait_recv()
    dst_pair[...] = dst_pair[...] + dst_part[:, :, pl.ds(c, 1)].reshape(2, 4, 16, 256)
    for t in range(NX):
        to = (base, row_of + 2 * t)

        @pl.when(jnp.logical_or(x != 3, t != 3))
        def _():
            remote(dst_pair.at[:, t], dst_x.at[x], dst_send.at[t], dst_recv.at[x], to).start()

    @pl.when(x == 3)
    def _():
        dst_x[3] = dst_pair[:, 3]

    def chunks(ref, n, sem):
        return pltpu.make_async_copy(ref.at[pl.ds(0, n)], ref.at[pl.ds(0, n)], sem)

    chunks(rel_xy, 31, recv.at[3]).wait()
    rel_z[pl.ds(z, 1)] = (rel_near[pl.ds(mine, 1)][0] + jnp.sum(rel_xy[...], axis=0))[None]
    for dz in z_offsets:
        where = at(lax.rem(z + dz, NZ), y, x, c)
        remote(rel_z.at[z], rel_z.at[z], send.at[8], recv.at[8], where).start()

    for copy in src_sends:
        copy.wait_recv()
    src_half[...] = (src_pair[:, pl.ds(x, 1)].reshape(2, 16, 256) + src_x[1]) + (src_x[2] + src_x[3])
    src_far = remote(src_half.at[1 - yh], src_y, send.at[9], recv.at[9], opposite)
    src_far.start()
    for t in range(NX):
        source = (lax.rem(b + NB - 3 + t, NB), row_of + 2 * t)

        @pl.when(jnp.logical_or(x != 3, t != 3))
        def _():
            remote(dst_pair.at[:, t], dst_x.at[t], dst_send.at[t], dst_recv.at[t], source).wait_recv()

    dst_x[0] = (dst_x[0] + dst_x[1]) + (dst_x[2] + dst_x[3])
    dst_far = remote(dst_x.at[0, 1 - yh], dst_y, send.at[10], recv.at[10], opposite)
    dst_far.start()
    load_rows.wait()
    load_state.wait()
    src_far.wait_recv()
    total = src_half[pl.ds(yh, 1)][0] + src_y[...]
    lane = lax.broadcasted_iota(jnp.int32, (16, 256), 1)
    line = lax.broadcasted_iota(jnp.int32, (16, 256), 0)
    old = jnp.sum(jnp.where(lane == line + g * 16, own_state[...], 0.0), axis=1, keepdims=True)
    fresh = old + jnp.sum(total * total, axis=1, keepdims=True) * (1.0 / 256.0)
    new_embed[...] = own_rows[...].astype(F32) - 0.5 * total / jnp.sqrt(fresh)
    lane16 = lax.broadcasted_iota(jnp.int32, (16, 16), 1)
    line16 = lax.broadcasted_iota(jnp.int32, (16, 16), 0)
    new_state[...] = jnp.sum(jnp.where(lane16 == line16, fresh, 0.0), axis=0, keepdims=True)
    dst_far.wait_recv()
    dest_out[...] = dst_x[0, pl.ds(yh, 1)].reshape(16, 256) + dst_y[...]

    chunks(rel_z, 15, recv.at[8]).wait()
    rel_out[pl.ds(c, 1), pl.ds(mine, 1)] = jnp.sum(rel_z[...], axis=0)[None, None]
    for dx, dy in offsets:
        _, where = plane(dx, dy)
        remote(rel_out.at[c, mine], rel_out.at[c, mine], send.at[11], all_recv.at[dx], where).start()
    for dx in (0, 1, 3, 2):
        chunks(rel_xy, 7 if dx == 0 else 8, all_recv.at[dx]).wait()
        group = pl.ds(lax.rem(x + NX - dx, NX) * NY, NY)
        remote(rel_out.at[c, group], rel_out.at[c, group], send.at[12], recv.at[12], sibling).start()
    rel_c.wait_send()
    src_c.wait_send()
    dst_c.wait_send()
    chunks(rel_xy, 31, send.at[3]).wait()
    chunks(rel_z, 15, send.at[8]).wait()
    chunks(rel_xy, 31, send.at[11]).wait()
    for copy in src_sends:
        copy.wait_send()
    for t in range(NX):

        @pl.when(jnp.logical_or(x != 3, t != 3))
        def _():
            remote(dst_pair.at[:, t], dst_x.at[x], dst_send.at[t], dst_recv.at[x], sibling).wait_send()

    src_far.wait_send()
    dst_far.wait_send()
    last = remote(rel_out.at[c], rel_out.at[c], send.at[12], recv.at[12], sibling)
    last.wait_send()
    remote(rel_out.at[1 - c], rel_out.at[1 - c], send.at[12], recv.at[12], sibling).wait_recv()


def finish_kernel(a, b, c, d, a_out, b_out, c_out, d_out, sem):
    copies = [
        pltpu.make_async_copy(held, out, sem.at[i])
        for i, (held, out) in enumerate(((d, d_out), (a, a_out), (c, c_out), (b, b_out)))
    ]
    for copy in copies:
        copy.start()
    for copy in copies:
        copy.wait()


def on_device(embed, state, relation, src_index, dst_index, rel_index, neg_index, counts):
    vmem = pl.BlockSpec(memory_space=pltpu.VMEM)
    hbm = pl.BlockSpec(memory_space=pltpu.HBM)
    dma = pltpu.SemaphoreType.DMA
    i32 = jnp.int32

    def params(**more):
        return pltpu.CompilerParams(vmem_limit_bytes=24 << 20, **more)

    def shape(dims, kind):
        return jax.ShapeDtypeStruct(dims, kind)

    embed, relation, src_index, dst_index, rel_index, neg_index, counts, state = (
        pltpu.with_memory_space_constraint(a, pltpu.HBM)
        for a in (embed, relation, src_index, dst_index, rel_index, neg_index, counts, state.reshape(1, 256))
    )
    passed = pl.pallas_call(
        exchange_kernel,
        out_shape=[
            shape((256, 256), BF16),
            shape((4, 4, 2, 128), i32),
            shape((1024, 256), F32),
            shape((1024, 256), F32),
            shape((256, 1024), BF16),
            shape((256, 2048), BF16),
            shape((2, 256, 1024), BF16),
        ],
        in_specs=[hbm] * 7,
        out_specs=[vmem] * 7,
        scratch_shapes=[
            pltpu.VMEM((256, 256), BF16),
            pltpu.VMEM((512, 256), F32),
            pltpu.VMEM((512, 768), BF16),
            pltpu.VMEM((4, 4, 2, 128), i32),
            pltpu.VMEM((1, 4), i32),
            pltpu.VMEM((4, 4, 2, 128), i32),
            dma((7,)),
            dma((3,)),
            dma((3,)),
            dma((2,)),
            dma((2,)),
        ],
        compiler_params=params(collective_id=0, has_side_effects=True),
        name="exchange",
    )(embed, relation, src_index, dst_index, rel_index, neg_index, counts)
    results = [
        shape((16, 256), F32),
        shape((1, 16), F32),
        shape((16, 256), F32),
        shape((2, 32, 8, 256), F32),
    ]
    found = pl.pallas_call(
        reduce_kernel,
        out_shape=results,
        in_specs=[vmem] * 7 + [hbm] * 2,
        out_specs=[vmem] * 4,
        scratch_shapes=[
            pltpu.VMEM((1024, 512), BF16),
            pltpu.VMEM((2048, 512), BF16),
            pltpu.VMEM((1024, 512), BF16),
            pltpu.VMEM((16, 256), BF16),
            pltpu.VMEM((1, 256), F32),
            pltpu.VMEM((32, 8, 256), F32),
            pltpu.VMEM((32, 8, 256), F32),
            pltpu.VMEM((2, 4, 2, 16, 256), F32),
            pltpu.VMEM((2, 4, 2, 16, 256), F32),
            pltpu.VMEM((32, 8, 256), F32),
            pltpu.VMEM((2, 4, 16, 256), F32),
            pltpu.VMEM((2, 4, 16, 256), F32),
            pltpu.VMEM((31, 8, 256), F32),
            pltpu.VMEM((16, 8, 256), F32),
            pltpu.VMEM((4, 2, 16, 256), F32),
            pltpu.VMEM((4, 2, 16, 256), F32),
            pltpu.VMEM((2, 16, 256), F32),
            pltpu.VMEM((16, 256), F32),
            pltpu.VMEM((16, 256), F32),
            dma((13,)),
            dma((13,)),
            dma((4,)),
            dma((4,)),
            dma((4,)),
            dma((2,)),
        ],
        compiler_params=params(collective_id=1, has_side_effects=True),
        name="reduce",
    )(*passed, embed, state)
    new_embed, new_state, dest, rel_grad = pl.pallas_call(
        finish_kernel,
        out_shape=results,
        in_specs=[vmem] * 4,
        out_specs=[hbm] * 4,
        scratch_shapes=[dma((4,))],
        name="finish",
    )(*found)
    return (new_embed, new_state.reshape(16), dest, rel_grad.reshape(512, 256))


def solution(mesh):
    return jax.shard_map(
        on_device,
        mesh=mesh,
        in_specs=(
            P("blk", None),
            P("blk"),
            P(),
            P("blk", "grp", None, None, None),
            P("blk", "grp", None, None, None),
            P("blk", "grp", None, None, None),
            P("blk", "grp", None, None, None),
            P("blk", "grp", None),
        ),
        out_specs=(P(("blk", "grp"), None), P(("blk", "grp")), P(("blk", "grp"), None), P()),
        check_vma=False,
    )
```

time: 81.1 us -> 74.1 us (0.914)
  local copies, waits for them, and re-layouts: 8.52 us -> 2.54 us
  Pallas kernels: 71.5 us -> 70.3 us
    unnamed x20 -> x8, local copies, waits for them, and re-layouts: 8.52 us -> 2.54 us
    pallas_call x3, Pallas kernels: 71.5 us -> 70.3 us  [the longest x1 41.5 us: on_device(): pl.pallas_call(reduce_kernel, out_shape=results, in_specs=[vmem] * 7 + [h...]
where the time goes in v2:
time: 74.1 us; the launch traced here: 73.5 us
  Pallas kernels  70.3 us (95%)
  local copies, waits for them, and re-layouts  2.54 us (3%)
    pallas_call x1, Pallas kernels, on_device(): pl.pallas_call(reduce_kernel, out_shape=results, in_specs=[vmem] * 7 + [h...  41.5 us
    pallas_call x1, Pallas kernels, on_device(): pl.pallas_call(exchange_kernel, out_shape=[shape((256, 256), BF16), shape...  26.9 us
    unnamed x8, local copies, waits for them, and re-layouts  2.54 us
    pallas_call x1, Pallas kernels, on_device(): pl.pallas_call(finish_kernel, out_shape=results, in_specs=[vmem] * 4, out...  1.91 us

profile of v2, /device:TPU:1, one launch (start us, length us, event | category | flops | bytes accessed | tf_op | source)
XLA Modules:
  0.0 73.5 jit_solution(9061766404770381133)
XLA Ops:
  0.6 26.9 %exchange.1 = (bf16[256,256]{1,0:T(8,128)(2,1)S(1)}, s32[4,4,2,128]{3,2,1,0:T(2,128)S(1)}, f32[1024,256]{1,0:T(8,128)S(1)}, f32[1024,256]{1,0:T(8,128)S(1)}, bf1...) custom-call(bf16[256,256]{1,0:T(8,128)(2,1)} %embed.3, ...), custom_call_target="tpu_custom_call" | custom-call | tf_op jit(solution)/shard_map/exchange/pallas_call | solution.py:429
  27.6 41.5 %reduce.1 = (f32[16,256]{1,0:T(8,128)S(1)}, f32[1,16]{1,0:T(1,128)S(1)}, f32[16,256]{1,0:T(8,128)S(1)}, f32[2,32,8,256]{3,2,1,0:T(8,128)S(1)}) custom-call(bf16[256,256]{1,0:T(8,128)(2,1)S(1)} %get-tuple-element.19.slab, s32[4,4,2,128]{3,2,1,0:T(2,128)S(1)} %get-tuple-element.20.index, f32[1024,256]{1,0:T(8,128)S(1)} %get-tuple-element.21.src_rows, ...), custom_call_target="tpu_custom_call" | custom-call | tf_op jit(solution)/shard_map/reduce/pallas_call | solution.py:464
  69.0 0.0 copy-start
  69.1 0.8 %copy-done = f32[2,32,8,256]{3,2,1,0:T(8,128)} copy-done((f32[2,32,8,256]{3,2,1,0:T(8,128)}, f32[2,32,8,256]{3,2,1,0:T(8,128)S(1)}, u32[]{:S(2)}) %copy-start) | copy-done | bytes 524312
  69.8 0.0 copy-start.1
  69.8 0.6 copy-done.1
  70.4 0.0 copy-start.2
  70.4 0.6 copy-done.2
  71.0 0.0 copy-start.3
  71.0 0.6 copy-done.3
  71.6 1.9 %finish.1 = (f32[16,256]{1,0:T(8,128)}, f32[1,16]{1,0:T(1,128)}, f32[16,256]{1,0:T(8,128)}, f32[2,32,8,256]{3,2,1,0:T(8,128)}) custom-call(f32[16,256]{1,0:T(8,128)} %copy-done.1, f32[1,16]{1,0:T(1,128)} %copy-done.3, f32[16,256]{1,0:T(8,128)} %copy-done.2, f32[2,32,8,256]{3,2,1,0:T(8,128)} %copy-done), custom_call_target="tpu_custom_call" | custom-call | tf_op jit(solution)/shard_map/finish/pallas_call | solution.py:499
Async XLA Ops:
  69.0 0.8 %copy-start = (f32[2,32,8,256]{3,2,1,0:T(8,128)}, f32[2,32,8,256]{3,2,1,0:T(8,128)S(1)}, u32[]{:S(2)}) copy-start(f32[2,32,8,256]{3,2,1,0:T(8,128)S(1)} %get-tuple-element.29.d) | copy-start | bytes 1572868
  69.8 0.6 copy-start.1
  70.4 0.6 copy-start.2
  71.0 0.6 copy-start.3

commit v3 on v2

--- a/solution.py
+++ b/solution.py
@@ -100,7 +100,6 @@
 
     @pl.when(x > 0)
     def _():
-        greet(ahead)
         greet(behind)
 
     for copy in loads:
@@ -113,23 +112,21 @@
         for i in range(1, 4):
             packed[t, i] = loaded[i, t]
     load_own.wait()
-    pl.semaphore_wait(pltpu.get_barrier_semaphore(), jnp.where(x > 0, NX + 2, NX))
+    pl.semaphore_wait(pltpu.get_barrier_semaphore(), jnp.where(x > 0, NX + 1, NX))
 
     half = pl.ds(pl.multiple_of(c * 128, 128), 128)
     other = pl.ds(pl.multiple_of((1 - c) * 128, 128), 128)
-
-    sends = []
-    for d in (2, 1, 3):
-        there = lax.rem(x + d, NX)
-        copy = remote(packed.at[there], index.at[x], idx_send.at[d - 1], idx_recv.at[d - 1], at(z, y, there, c))
-        copy.start()
-        sends.append(copy)
 
     @pl.when(x > 0)
     def _():
         remote(own.at[half], slab.at[half], slab_send.at[0], slab_recv.at[0], ahead).start()
 
-    index[pl.ds(x, 1)] = packed[pl.ds(x, 1)]
+    sends = {}
+    for d in (2, 1, 3):
+        there = lax.rem(x + d, NX)
+        sends[d] = remote(packed.at[there], index.at[d], idx_send.at[d - 1], idx_recv.at[d - 1], at(z, y, there, c))
+        sends[d].start()
+    index[0:1] = packed[pl.ds(x, 1)]
 
     @pl.when(x == 0)
     def _():
@@ -143,23 +140,22 @@
     parts[:, 0:256] = high
     parts[:, 256:512] = middle
     parts[:, 512:768] = (rest - middle.astype(F32)).astype(BF16)
-    for copy in sends:
-        copy.wait()
-
     lane = lax.broadcasted_iota(jnp.int32, (256, 256), 1)
     lane_r = lax.broadcasted_iota(jnp.int32, (256, 512), 1)
     sub = lax.broadcasted_iota(jnp.int32, (256, 256), 0)
     sub_r = lax.broadcasted_iota(jnp.int32, (2, 256, 256), 0) * 256 + lax.broadcasted_iota(jnp.int32, (2, 256, 256), 1)
-    for k in range(NX):
+    for k, d in enumerate((0, 1, 3, 2)):
         edges = slice(k * 256, k * 256 + 256)
         negs = slice(1024 + k * 256, 1024 + k * 256 + 256)
-        src_rows[edges] = dot(hot(lane == columns_of(index[k, 0])), own[...])
-        pieces = dot(hot(lane_r == columns_of(index[k, 2])), parts[...])
+        if d > 0:
+            sends[d].wait_recv()
+        src_rows[edges] = dot(hot(lane == columns_of(index[d, 0])), own[...])
+        pieces = dot(hot(lane_r == columns_of(index[d, 2])), parts[...])
         rel_rows[edges] = (pieces[:, 0:256] + pieces[:, 256:512]) + pieces[:, 512:768]
-        hot_src[:, edges] = hot(sub == line_of(index[k, 0]))
-        hot_dst[:, edges] = hot(sub == line_of(index[k, 1]))
-        hot_dst[:, negs] = hot(sub == line_of(index[k, 3]))
-        hot_rel[:, :, edges] = hot(sub_r == line_of(index[k, 2])[None])
+        hot_src[:, edges] = hot(sub == line_of(index[d, 0]))
+        hot_dst[:, edges] = hot(sub == line_of(index[d, 1]))
+        hot_dst[:, negs] = hot(sub == line_of(index[d, 3]))
+        hot_rel[:, :, edges] = hot(sub_r == line_of(index[d, 2])[None])
 
     @pl.when(x > 0)
     def _():
@@ -171,6 +167,9 @@
         second.wait_send()
         remote(slab.at[other], slab.at[other], slab_send.at[1], slab_recv.at[1], sibling).wait_recv()
 
+    for d in (1, 2, 3):
+        sends[d].wait_send()
+
 
 def bucket_gradients(index, slab, src_rows, rel_rows, g_src, g_dst, g_rel):
     def split(ref, rows, value):
@@ -179,13 +178,13 @@
         ref[rows, 256:512] = (value - top.astype(F32)).astype(BF16)
 
     lane = lax.broadcasted_iota(jnp.int32, (256, 256), 1)
-    for k in range(NX):
+    for k, d in enumerate((0, 1, 3, 2)):
         edges = slice(k * 256, k * 256 + 256)
         negs = slice(1024 + k * 256, 1024 + k * 256 + 256)
         src_v = src_rows[edges]
         rel_v = rel_rows[edges]
-        dst_v = dot(hot(lane == columns_of(index[k, 1])), slab[...])
-        neg_v = dot(hot(lane == columns_of(index[k, 3])), slab[...]).astype(BF16)
+        dst_v = dot(hot(lane == columns_of(index[d, 1])), slab[...])
+        neg_v = dot(hot(lane == columns_of(index[d, 3])), slab[...]).astype(BF16)
         scaled = src_v * rel_v
         positive = jnp.sum(scaled * dst_v, axis=1, keepdims=True)
         pos_grad = -jax.nn.sigmoid(-positive)
@@ -272,12 +271,10 @@
     for dx, dy in offsets:
         greet(plane(dx, dy)[1])
     for t in range(NX):
-        to = (base, row_of + 2 * t)
         source = (lax.rem(b + NB - 3 + t, NB), row_of + 2 * t)
 
         @pl.when(jnp.logical_or(x != 3, t != 3))
         def _():
-            greet(to)
             greet(source)
 
     greet(sibling)
@@ -288,7 +285,7 @@
 
     bucket_gradients(index, slab, src_rows, rel_rows, g_src, g_dst, g_rel)
     rel_far[...] = both_terms(hot_rel[pl.ds(1 - c, 1)][0], g_rel[...]).reshape(32, 8, 256)
-    pl.semaphore_wait(pltpu.get_barrier_semaphore(), 1 + 15 + 31 + jnp.where(x == 3, 6, 8))
+    pl.semaphore_wait(pltpu.get_barrier_semaphore(), 1 + 15 + 31 + jnp.where(x == 3, 3, 4))
 
     def pair(source, target, i):
         return remote(source, target, send.at[i], recv.at[i], sibling)
@@ -305,10 +302,33 @@
         chunk, where = plane(dx, dy)
         remote(rel_near.at[chunk], rel_xy.at[i], send.at[3], recv.at[3], where).start()
 
-    src_part[...] = both_terms(hot_src[...], g_src[...]).reshape(2, 4, 2, 16, 256)
-    src_c.start()
     dst_part[...] = both_terms(hot_dst[...], g_dst[...]).reshape(2, 4, 2, 16, 256)
     dst_c.start()
+    src_part[...] = both_terms(hot_src[...], g_src[...]).reshape(2, 4, 2, 16, 256)
+    dst_c.wait_recv()
+    dst_pair[...] = dst_pair[...] + dst_part[:, :, pl.ds(c, 1)].reshape(2, 4, 16, 256)
+    for t in range(NX):
+        to = (base, row_of + 2 * t)
+
+        @pl.when(jnp.logical_or(x != 3, t != 3))
+        def _():
+            remote(dst_pair.at[:, t], dst_x.at[x], dst_send.at[t], dst_recv.at[x], to).start()
+
+    @pl.when(x == 3)
+    def _():
+        dst_x[3] = dst_pair[:, 3]
+
+    src_c.start()
+
+    def chunks(ref, n, sem):
+        return pltpu.make_async_copy(ref.at[pl.ds(0, n)], ref.at[pl.ds(0, n)], sem)
+
+    chunks(rel_xy, 31, recv.at[3]).wait()
+    rel_z[pl.ds(z, 1)] = (rel_near[pl.ds(mine, 1)][0] + jnp.sum(rel_xy[...], axis=0))[None]
+    for dz in z_offsets:
+        where = at(lax.rem(z + dz, NZ), y, x, c)
+        remote(rel_z.at[z], rel_z.at[z], send.at[8], recv.at[8], where).start()
+
     src_c.wait_recv()
     src_pair[...] = src_pair[...] + src_part[:, :, pl.ds(c, 1)].reshape(2, 4, 16, 256)
     src_sends = []
@@ -317,28 +337,6 @@
         copy = remote(src_pair.at[:, px], src_x.at[d], send.at[4 + d], recv.at[4 + d], at(z, y, px, c))
         copy.start()
         src_sends.append(copy)
-    dst_c.wait_recv()
-    dst_pair[...] = dst_pair[...] + dst_part[:, :, pl.ds(c, 1)].reshape(2, 4, 16, 256)
-    for t in range(NX):
-        to = (base, row_of + 2 * t)
-
-        @pl.when(jnp.logical_or(x != 3, t != 3))
-        def _():
-            remote(dst_pair.at[:, t], dst_x.at[x], dst_send.at[t], dst_recv.at[x], to).start()
-
-    @pl.when(x == 3)
-    def _():
-        dst_x[3] = dst_pair[:, 3]
-
-    def chunks(ref, n, sem):
-        return pltpu.make_async_copy(ref.at[pl.ds(0, n)], ref.at[pl.ds(0, n)], sem)
-
-    chunks(rel_xy, 31, recv.at[3]).wait()
-    rel_z[pl.ds(z, 1)] = (rel_near[pl.ds(mine, 1)][0] + jnp.sum(rel_xy[...], axis=0))[None]
-    for dz in z_offsets:
-        where = at(lax.rem(z + dz, NZ), y, x, c)
-        remote(rel_z.at[z], rel_z.at[z], send.at[8], recv.at[8], where).start()
-
     for copy in src_sends:
         copy.wait_recv()
     src_half[...] = (src_pair[:, pl.ds(x, 1)].reshape(2, 16, 256) + src_x[1]) + (src_x[2] + src_x[3])
@@ -354,6 +352,11 @@
     dst_x[0] = (dst_x[0] + dst_x[1]) + (dst_x[2] + dst_x[3])
     dst_far = remote(dst_x.at[0, 1 - yh], dst_y, send.at[10], recv.at[10], opposite)
     dst_far.start()
+    chunks(rel_z, 15, recv.at[8]).wait()
+    rel_out[pl.ds(c, 1), pl.ds(mine, 1)] = jnp.sum(rel_z[...], axis=0)[None, None]
+    for dx, dy in offsets:
+        _, where = plane(dx, dy)
+        remote(rel_out.at[c, mine], rel_out.at[c, mine], send.at[11], all_recv.at[dx], where).start()
     load_rows.wait()
     load_state.wait()
     src_far.wait_recv()
@@ -366,18 +369,12 @@
     lane16 = lax.broadcasted_iota(jnp.int32, (16, 16), 1)
     line16 = lax.broadcasted_iota(jnp.int32, (16, 16), 0)
     new_state[...] = jnp.sum(jnp.where(lane16 == line16, fresh, 0.0), axis=0, keepdims=True)
-    dst_far.wait_recv()
-    dest_out[...] = dst_x[0, pl.ds(yh, 1)].reshape(16, 256) + dst_y[...]
-
-    chunks(rel_z, 15, recv.at[8]).wait()
-    rel_out[pl.ds(c, 1), pl.ds(mine, 1)] = jnp.sum(rel_z[...], axis=0)[None, None]
-    for dx, dy in offsets:
-        _, where = plane(dx, dy)
-        remote(rel_out.at[c, mine], rel_out.at[c, mine], send.at[11], all_recv.at[dx], where).start()
     for dx in (0, 1, 3, 2):
         chunks(rel_xy, 7 if dx == 0 else 8, all_recv.at[dx]).wait()
         group = pl.ds(lax.rem(x + NX - dx, NX) * NY, NY)
         remote(rel_out.at[c, group], rel_out.at[c, group], send.at[12], recv.at[12], sibling).start()
+    dst_far.wait_recv()
+    dest_out[...] = dst_x[0, pl.ds(yh, 1)].reshape(16, 256) + dst_y[...]
     rel_c.wait_send()
     src_c.wait_send()
     dst_c.wait_send()
@@ -502,6 +499,7 @@
         in_specs=[vmem] * 4,
         out_specs=[hbm] * 4,
         scratch_shapes=[dma((4,))],
+        compiler_params=pltpu.CompilerParams(vmem_limit_bytes=4 << 20),
         name="finish",
     )(*found)
     return (new_embed, new_state.reshape(16), dest, rel_grad.reshape(512, 256))

time: 74.1 us -> 69.3 us (0.935)
  local copies, waits for them, and re-layouts: 2.54 us -> 0 us
  Pallas kernels: 70.3 us -> 68.4 us
    pallas_call x1, Pallas kernels: 26.9 us -> 19.4 us  [on_device(): pl.pallas_call(exchange_kernel, out_shape=[shape((256, 256), BF16), shape...]
    pallas_call x1, Pallas kernels: 41.5 us -> 48.2 us  [on_device(): pl.pallas_call(reduce_kernel, out_shape=results, in_specs=[vmem] * 7 + [h...]
    unnamed x8 -> x0, local copies, waits for them, and re-layouts: 2.54 us -> none
    pallas_call x1, Pallas kernels: 1.91 us -> 0.84 us  [on_device(): pl.pallas_call(finish_kernel, out_shape=results, in_specs=[vmem] * 4, out...]
where the time goes in v3:
time: 69.3 us; the launch traced here: 69.1 us
  Pallas kernels  68.4 us (99%)
    pallas_call x1, Pallas kernels, on_device(): pl.pallas_call(reduce_kernel, out_shape=results, in_specs=[vmem] * 7 + [h...  48.2 us
    pallas_call x1, Pallas kernels, on_device(): pl.pallas_call(exchange_kernel, out_shape=[shape((256, 256), BF16), shape...  19.4 us

profile of v3, /device:TPU:1, one launch (start us, length us, event | category | flops | bytes accessed | tf_op | source)
XLA Modules:
  0.0 69.1 jit_solution(14363976517251646371)
XLA Ops:
  0.6 19.4 %exchange.1 = (bf16[256,256]{1,0:T(8,128)(2,1)S(1)}, s32[4,4,2,128]{3,2,1,0:T(2,128)S(1)}, f32[1024,256]{1,0:T(8,128)S(1)}, f32[1024,256]{1,0:T(8,128)S(1)}, bf1...) custom-call(bf16[256,256]{1,0:T(8,128)(2,1)} %embed.3, ...), custom_call_target="tpu_custom_call" | custom-call | tf_op jit(solution)/shard_map/exchange/pallas_call | solution.py:426
  20.0 48.2 %reduce.1 = (f32[16,256]{1,0:T(8,128)S(1)}, f32[1,16]{1,0:T(1,128)S(1)}, f32[16,256]{1,0:T(8,128)S(1)}, f32[2,32,8,256]{3,2,1,0:T(8,128)S(1)}) custom-call(bf16[256,256]{1,0:T(8,128)(2,1)S(1)} %get-tuple-element.19.slab, s32[4,4,2,128]{3,2,1,0:T(2,128)S(1)} %get-tuple-element.20.index, f32[1024,256]{1,0:T(8,128)S(1)} %get-tuple-element.21.src_rows, ...), custom_call_target="tpu_custom_call" | custom-call | tf_op jit(solution)/shard_map/reduce/pallas_call | solution.py:461
  68.2 0.8 %finish.1 = (f32[16,256]{1,0:T(8,128)}, f32[1,16]{1,0:T(1,128)}, f32[16,256]{1,0:T(8,128)}, f32[2,32,8,256]{3,2,1,0:T(8,128)}) custom-call(f32[16,256]{1,0:T(8,128)S(1)} %get-tuple-element.26.a, f32[1,16]{1,0:T(1,128)S(1)} %get-tuple-element.27.b, f32[16,256]{1,0:T(8,128)S(1)} %get-tuple-element.28.c, f32[2,32,8,256]{3,2,1,0:T(8,128)S(1)} %get-tuple-element.29.d), custom_call_target="tpu_custom_call" | custom-call | tf_op jit(solution)/shard_map/finish/pallas_call | solution.py:496

commit v4 on v3

v4 whole, which is shorter than its diff:
```python
import jax
import jax.numpy as jnp
from jax import lax
from jax.experimental import pallas as pl
from jax.experimental.pallas import tpu as pltpu
from jax.sharding import PartitionSpec as P

NZ = 16
NX = 4
NY = 8
NB = 64
MESH = pl.DeviceIdType.MESH
F32 = jnp.float32
BF16 = jnp.bfloat16


def position():
    b = lax.axis_index("blk")
    g = lax.axis_index("grp")
    z = lax.rem(b, NZ)
    y = lax.div(g, 8) * 4 + lax.div(b, NZ)
    x = lax.rem(lax.div(g, 2), NX)
    c = lax.rem(g, 2)
    return b, g, z, y, x, c


def at(z, y, x, c):
    return (lax.rem(y, 4) * NZ + z, lax.div(y, 4) * 8 + x * 2 + c)


def remote(src, dst, send, recv, where):
    return pltpu.make_async_remote_copy(
        src_ref=src, dst_ref=dst, send_sem=send, recv_sem=recv, device_id=where, device_id_type=MESH
    )


def greet(where):
    pl.semaphore_signal(pltpu.get_barrier_semaphore(), inc=1, device_id=where, device_id_type=MESH)


def dot(a, b):
    return jnp.dot(a, b, preferred_element_type=F32)


def hot(hit):
    return jnp.where(hit, 1.0, 0.0).astype(BF16)


def columns_of(rows):
    turned = rows.T
    return jnp.concatenate([turned[:, 0:1], turned[:, 1:2]], axis=0)


def line_of(rows):
    return jnp.concatenate([rows[0:1], rows[1:2]], axis=1)


def bucket_gradients(index, slab, src_rows, rel_rows, g_src, g_dst, g_rel):
    def split(ref, rows, value):
        top = value.astype(BF16)
        ref[rows, 0:256] = top
        ref[rows, 256:512] = (value - top.astype(F32)).astype(BF16)

    lane = lax.broadcasted_iota(jnp.int32, (256, 256), 1)
    for k, d in enumerate((0, 1, 3, 2)):
        edges = slice(k * 256, k * 256 + 256)
        negs = slice(1024 + k * 256, 1024 + k * 256 + 256)
        src_v = src_rows[edges]
        rel_v = rel_rows[edges]
        dst_v = dot(hot(lane == columns_of(index[d, 1])), slab[...])
        neg_v = dot(hot(lane == columns_of(index[d, 3])), slab[...]).astype(BF16)
        scaled = src_v * rel_v
        positive = jnp.sum(scaled * dst_v, axis=1, keepdims=True)
        pos_grad = -jax.nn.sigmoid(-positive)
        scaled_b = scaled.astype(BF16)
        from_neg = []
        neg_g = []
        for j in range(2):
            block = slice(j * 128, j * 128 + 128)
            s, n = scaled_b[block], neg_v[block]
            score = lax.dot_general(s, n, (((1,), (1,)), ((), ())), preferred_element_type=F32)
            weight = (jax.nn.sigmoid(score) * (1.0 / 128.0)).astype(BF16)
            from_neg.append(dot(weight, n))
            neg_g.append(lax.dot_general(weight, s, (((0,), (0,)), ((), ())), preferred_element_type=F32))
        scaled_grad = pos_grad * dst_v + jnp.concatenate(from_neg, axis=0)
        split(g_rel, edges, scaled_grad * src_v)
        split(g_src, edges, scaled_grad * rel_v)
        split(g_dst, edges, pos_grad * scaled)
        split(g_dst, negs, jnp.concatenate(neg_g, axis=0))


def both_terms(h, g):
    both = dot(h, g)
    return both[:, 0:256] + both[:, 256:512]


def window_kernel(
    embed,
    relation,
    src,
    dst,
    rel,
    neg,
    counts,
    state,
    new_embed,
    new_state,
    dest_out,
    rel_out,
    slab,
    index,
    src_rows,
    rel_rows,
    hot_src,
    hot_dst,
    hot_rel,
    own,
    table,
    parts,
    loaded,
    live,
    packed,
    g_src,
    g_dst,
    g_rel,
    own_state,
    rel_far,
    rel_near,
    src_part,
    dst_part,
    rel_pair,
    src_pair,
    dst_pair,
    rel_xy,
    rel_z,
    src_x,
    dst_x,
    src_half,
    src_y,
    dst_y,
    load_sem,
    idx_send,
    idx_recv,
    slab_send,
    slab_recv,
    send,
    recv,
    dst_send,
    dst_recv,
    pair_recv,
    all_recv,
    here,
):
    b, g, z, y, x, c = position()
    loads = [pltpu.make_async_copy(ref.at[0, 0], loaded.at[i], load_sem.at[i]) for i, ref in enumerate((src, dst, rel, neg))]
    loads.append(pltpu.make_async_copy(counts.at[0], live, load_sem.at[4]))
    load_own = pltpu.make_async_copy(embed, own, load_sem.at[5])
    load_table = pltpu.make_async_copy(relation, table, load_sem.at[6])
    load_state = pltpu.make_async_copy(state, own_state, load_sem.at[7])
    for copy in loads:
        copy.start()
    load_own.start()
    load_table.start()
    load_state.start()

    sibling = (b, g + 1 - 2 * c)
    ahead = (lax.rem(b + x, NB), g)
    behind = (lax.rem(b + NB - x, NB), g)
    opposite = at(z, lax.rem(y + 4, NY), x, c)
    yh = lax.div(y, 4)
    base = lax.rem(b + 3 + NB - x, NB)
    row_of = lax.div(g, 8) * 8 + c
    mine = x * NY + y

    y_order = (4, 3, 5, 2, 6, 1, 7, 0)
    z_offsets = (8, 7, 9, 6, 10, 5, 11, 4, 12, 3, 13, 2, 14, 1, 15)

    def plane(dx, dy):
        px, py = lax.rem(x + dx, NX), lax.rem(y + dy, NY)
        return px * NY + py, at(z, py, px, c)

    def along_x(d):
        return at(z, y, lax.rem(x + d, NX), c)

    def along_y(d):
        return at(z, lax.rem(y + NY + d, NY), x, c)

    def along_z(d):
        return at(lax.rem(z + NZ + d, NZ), y, x, c)

    def tell(i, *wheres):
        for where in wheres:
            pl.semaphore_signal(here.at[i], inc=1, device_id=where, device_id_type=MESH)

    greet(sibling)
    for d in (2, 1, 3):
        greet(along_x(d))
    for d in (1, -1):
        greet(along_y(d))
        greet(along_z(d))

    @pl.when(x > 0)
    def _():
        greet(behind)

    for copy in loads:
        copy.wait()
    blocks = lax.broadcasted_iota(jnp.int32, (2, 128), 0)
    spots = lax.broadcasted_iota(jnp.int32, (1, 4), 1)
    for t in range(NX):
        count = jnp.sum(jnp.where(spots == t, live[...], 0), axis=1, keepdims=True)
        packed[t, 0] = jnp.where(blocks < count, loaded[0, t], -1)
        for i in range(1, 4):
            packed[t, i] = loaded[i, t]
    load_own.wait()
    pl.semaphore_wait(pltpu.get_barrier_semaphore(), jnp.where(x > 0, 9, 8))

    half = pl.ds(pl.multiple_of(c * 128, 128), 128)
    other = pl.ds(pl.multiple_of((1 - c) * 128, 128), 128)

    @pl.when(x > 0)
    def _():
        remote(own.at[half], slab.at[half], slab_send.at[0], slab_recv.at[0], ahead).start()

    sends = {}
    for d in (2, 1, 3):
        there = lax.rem(x + d, NX)
        sends[d] = remote(packed.at[there], index.at[d], idx_send.at[d - 1], idx_recv.at[d - 1], along_x(d))
        sends[d].start()
    tell(0, along_y(1), along_y(-1))
    tell(1, along_z(1), along_z(-1))
    index[0:1] = packed[pl.ds(x, 1)]

    @pl.when(x == 0)
    def _():
        slab[...] = own[...]

    load_table.wait()
    r = table[...]
    high = r.astype(BF16)
    rest = r - high.astype(F32)
    middle = rest.astype(BF16)
    parts[:, 0:256] = high
    parts[:, 256:512] = middle
    parts[:, 512:768] = (rest - middle.astype(F32)).astype(BF16)

    lane = lax.broadcasted_iota(jnp.int32, (256, 256), 1)
    lane_r = lax.broadcasted_iota(jnp.int32, (256, 512), 1)
    sub = lax.broadcasted_iota(jnp.int32, (256, 256), 0)
    sub_r = lax.broadcasted_iota(jnp.int32, (2, 256, 256), 0) * 256 + lax.broadcasted_iota(jnp.int32, (2, 256, 256), 1)
    for k, d in enumerate((0, 1, 3, 2)):
        edges = slice(k * 256, k * 256 + 256)
        negs = slice(1024 + k * 256, 1024 + k * 256 + 256)
        if k == 1:
            pl.semaphore_wait(here.at[0], 2)
            pl.semaphore_wait(here.at[1], 2)
            tell(2, along_y(2), along_y(-2))
            tell(3, along_z(2), along_z(-2))
        if k == 2:
            pl.semaphore_wait(here.at[2], 2)
            pl.semaphore_wait(here.at[3], 2)
            tell(4, along_x(2), along_x(1), along_x(3))
            tell(5, along_z(4), along_z(-4))
        if k == 3:
            pl.semaphore_wait(here.at[4], 3)

            @pl.when(x < 3)
            def _():
                tell(6, along_z(x - 3))

        if d > 0:
            sends[d].wait_recv()
        src_rows[edges] = dot(hot(lane == columns_of(index[d, 0])), own[...])
        pieces = dot(hot(lane_r == columns_of(index[d, 2])), parts[...])
        rel_rows[edges] = (pieces[:, 0:256] + pieces[:, 256:512]) + pieces[:, 512:768]
        hot_src[:, edges] = hot(sub == line_of(index[d, 0]))
        hot_dst[:, edges] = hot(sub == line_of(index[d, 1]))
        hot_dst[:, negs] = hot(sub == line_of(index[d, 3]))
        hot_rel[:, :, edges] = hot(sub_r == line_of(index[d, 2])[None])

    @pl.when(x > 0)
    def _():
        first = remote(own.at[half], slab.at[half], slab_send.at[0], slab_recv.at[0], ahead)
        second = remote(slab.at[half], slab.at[half], slab_send.at[1], slab_recv.at[1], sibling)
        first.wait_recv()
        second.start()
        first.wait_send()
        second.wait_send()
        remote(slab.at[other], slab.at[other], slab_send.at[1], slab_recv.at[1], sibling).wait_recv()

    for d in (1, 2, 3):
        sends[d].wait_send()

    bucket_gradients(index, slab, src_rows, rel_rows, g_src, g_dst, g_rel)
    rel_far[...] = both_terms(hot_rel[pl.ds(1 - c, 1)][0], g_rel[...]).reshape(32, 8, 256)

    def pair(source, target, i):
        return remote(source, target, send.at[i], recv.at[i], sibling)

    src_c = pair(src_part.at[:, :, 1 - c], src_pair, 1)
    dst_c = pair(dst_part.at[:, :, 1 - c], dst_pair, 2)

    rel_c = {}
    for dx in (2, 1, 3, 0):
        rows = pl.ds(lax.rem(x + dx, NX) * NY, NY)
        mirror = pl.ds(lax.rem(x + dx, NX) * NY, NY)
        rel_c[dx] = remote(rel_far.at[rows], rel_pair.at[mirror], send.at[0], pair_recv.at[dx], sibling)
        rel_c[dx].start()
    rel_near[...] = both_terms(hot_rel[pl.ds(c, 1)][0], g_rel[...]).reshape(32, 8, 256)
    for dx in (2, 1, 3, 0):
        rows = pl.ds(lax.rem(x + dx, NX) * NY, NY)
        rel_c[dx].wait_recv()
        rel_near[rows] = rel_near[rows] + rel_pair[rows]
        for dy in y_order:
            if (dx, dy) != (0, 0):
                chunk, where = plane(dx, dy)
                remote(rel_near.at[chunk], rel_xy.at[(dx * NY + dy) - 1], send.at[3], recv.at[3], where).start()

    dst_part[...] = both_terms(hot_dst[...], g_dst[...]).reshape(2, 4, 2, 16, 256)
    dst_c.start()
    src_part[...] = both_terms(hot_src[...], g_src[...]).reshape(2, 4, 2, 16, 256)
    dst_c.wait_recv()
    dst_pair[...] = dst_pair[...] + dst_part[:, :, pl.ds(c, 1)].reshape(2, 4, 16, 256)
    @pl.when(x < 3)
    def _():
        pl.semaphore_wait(here.at[6], 1)

    for t in range(NX):
        to = (base, row_of + 2 * t)

        @pl.when(jnp.logical_or(x != 3, t != 3))
        def _():
            remote(dst_pair.at[:, t], dst_x.at[x], dst_send.at[t], dst_recv.at[x], to).start()

    @pl.when(x == 3)
    def _():
        dst_x[3] = dst_pair[:, 3]

    src_c.start()

    offsets = [(dx, dy) for dx in (2, 1, 3, 0) for dy in y_order if (dx, dy) != (0, 0)]

    def chunks(ref, n, sem):
        return pltpu.make_async_copy(ref.at[pl.ds(0, n)], ref.at[pl.ds(0, n)], sem)

    chunks(rel_xy, 31, recv.at[3]).wait()
    rel_z[pl.ds(z, 1)] = (rel_near[pl.ds(mine, 1)][0] + jnp.sum(rel_xy[...], axis=0))[None]
    pl.semaphore_wait(here.at[5], 2)
    for dz in z_offsets:
        where = along_z(dz)
        remote(rel_z.at[z], rel_z.at[z], send.at[8], recv.at[8], where).start()

    src_c.wait_recv()
    src_pair[...] = src_pair[...] + src_part[:, :, pl.ds(c, 1)].reshape(2, 4, 16, 256)
    src_sends = []
    for d in (2, 1, 3):
        px = lax.rem(x + d, NX)
        copy = remote(src_pair.at[:, px], src_x.at[d], send.at[4 + d], recv.at[4 + d], at(z, y, px, c))
        copy.start()
        src_sends.append(copy)
    for copy in src_sends:
        copy.wait_recv()
    src_half[...] = (src_pair[:, pl.ds(x, 1)].reshape(2, 16, 256) + src_x[1]) + (src_x[2] + src_x[3])
    src_far = remote(src_half.at[1 - yh], src_y, send.at[9], recv.at[9], opposite)
    src_far.start()
    for t in range(NX):
        source = (lax.rem(b + NB - 3 + t, NB), row_of + 2 * t)

        @pl.when(jnp.logical_or(x != 3, t != 3))
        def _():
            remote(dst_pair.at[:, t], dst_x.at[t], dst_send.at[t], dst_recv.at[t], source).wait_recv()

    dst_x[0] = (dst_x[0] + dst_x[1]) + (dst_x[2] + dst_x[3])
    dst_far = remote(dst_x.at[0, 1 - yh], dst_y, send.at[10], recv.at[10], opposite)
    dst_far.start()
    chunks(rel_z, 15, recv.at[8]).wait()
    rel_out[pl.ds(c, 1), pl.ds(mine, 1)] = jnp.sum(rel_z[...], axis=0)[None, None]
    for dx, dy in offsets:
        _, where = plane(dx, dy)
        remote(rel_out.at[c, mine], rel_out.at[c, mine], send.at[11], all_recv.at[dx], where).start()
    load_state.wait()
    src_far.wait_recv()
    total = src_half[pl.ds(yh, 1)][0] + src_y[...]
    lane = lax.broadcasted_iota(jnp.int32, (16, 256), 1)
    line = lax.broadcasted_iota(jnp.int32, (16, 256), 0)
    old = jnp.sum(jnp.where(lane == line + g * 16, own_state[...], 0.0), axis=1, keepdims=True)
    fresh = old + jnp.sum(total * total, axis=1, keepdims=True) * (1.0 / 256.0)
    new_embed[...] = own[pl.ds(pl.multiple_of(g * 16, 16), 16)].astype(F32) - 0.5 * total / jnp.sqrt(fresh)
    lane16 = lax.broadcasted_iota(jnp.int32, (16, 16), 1)
    line16 = lax.broadcasted_iota(jnp.int32, (16, 16), 0)
    new_state[...] = jnp.sum(jnp.where(lane16 == line16, fresh, 0.0), axis=0, keepdims=True)
    for dx in (0, 1, 3, 2):
        chunks(rel_xy, 7 if dx == 0 else 8, all_recv.at[dx]).wait()
        group = pl.ds(lax.rem(x + NX - dx, NX) * NY, NY)
        remote(rel_out.at[c, group], rel_out.at[c, group], send.at[12], recv.at[12], sibling).start()
    dst_far.wait_recv()
    dest_out[...] = dst_x[0, pl.ds(yh, 1)].reshape(16, 256) + dst_y[...]
    remote(rel_far, rel_pair, send.at[0], recv.at[0], sibling).wait_send()
    src_c.wait_send()
    dst_c.wait_send()
    chunks(rel_xy, 31, send.at[3]).wait()
    chunks(rel_z, 15, send.at[8]).wait()
    chunks(rel_xy, 31, send.at[11]).wait()
    for copy in src_sends:
        copy.wait_send()
    for t in range(NX):

        @pl.when(jnp.logical_or(x != 3, t != 3))
        def _():
            remote(dst_pair.at[:, t], dst_x.at[x], dst_send.at[t], dst_recv.at[x], sibling).wait_send()

    src_far.wait_send()
    dst_far.wait_send()
    last = remote(rel_out.at[c], rel_out.at[c], send.at[12], recv.at[12], sibling)
    last.wait_send()
    remote(rel_out.at[1 - c], rel_out.at[1 - c], send.at[12], recv.at[12], sibling).wait_recv()


def finish_kernel(a, b, c, d, a_out, b_out, c_out, d_out, sem):
    copies = [
        pltpu.make_async_copy(held, out, sem.at[i])
        for i, (held, out) in enumerate(((d, d_out), (a, a_out), (c, c_out), (b, b_out)))
    ]
    for copy in copies:
        copy.start()
    for copy in copies:
        copy.wait()


def on_device(embed, state, relation, src_index, dst_index, rel_index, neg_index, counts):
    vmem = pl.BlockSpec(memory_space=pltpu.VMEM)
    hbm = pl.BlockSpec(memory_space=pltpu.HBM)
    dma = pltpu.SemaphoreType.DMA

    def held(dims, kind=F32):
        return pltpu.VMEM(dims, kind)

    results = [
        jax.ShapeDtypeStruct(dims, F32) for dims in ((16, 256), (1, 16), (16, 256), (2, 32, 8, 256))
    ]
    given = (embed, relation, src_index, dst_index, rel_index, neg_index, counts, state.reshape(1, 256))
    found = pl.pallas_call(
        window_kernel,
        out_shape=results,
        in_specs=[hbm] * 8,
        out_specs=[vmem] * 4,
        scratch_shapes=[
            held((256, 256), BF16),
            held((4, 4, 2, 128), jnp.int32),
            held((1024, 256)),
            held((1024, 256)),
            held((256, 1024), BF16),
            held((256, 2048), BF16),
            held((2, 256, 1024), BF16),
            held((256, 256), BF16),
            held((512, 256)),
            held((512, 768), BF16),
            held((4, 4, 2, 128), jnp.int32),
            held((1, 4), jnp.int32),
            held((4, 4, 2, 128), jnp.int32),
            held((1024, 512), BF16),
            held((2048, 512), BF16),
            held((1024, 512), BF16),
            held((1, 256)),
            held((32, 8, 256)),
            held((32, 8, 256)),
            held((2, 4, 2, 16, 256)),
            held((2, 4, 2, 16, 256)),
            held((32, 8, 256)),
            held((2, 4, 16, 256)),
            held((2, 4, 16, 256)),
            held((31, 8, 256)),
            held((16, 8, 256)),
            held((4, 2, 16, 256)),
            held((4, 2, 16, 256)),
            held((2, 16, 256)),
            held((16, 256)),
            held((16, 256)),
            dma((8,)),
            dma((3,)),
            dma((3,)),
            dma((2,)),
            dma((2,)),
            dma((13,)),
            dma((13,)),
            dma((4,)),
            dma((4,)),
            dma((4,)),
            dma((4,)),
            pltpu.SemaphoreType.REGULAR((7,)),
        ],
        compiler_params=pltpu.CompilerParams(
            vmem_limit_bytes=48 << 20, collective_id=0, has_side_effects=True
        ),
        name="window",
    )(*(pltpu.with_memory_space_constraint(a, pltpu.HBM) for a in given))
    new_embed, new_state, dest, rel_grad = pl.pallas_call(
        finish_kernel,
        out_shape=results,
        in_specs=[vmem] * 4,
        out_specs=[hbm] * 4,
        scratch_shapes=[dma((4,))],
        compiler_params=pltpu.CompilerParams(vmem_limit_bytes=4 << 20),
        name="finish",
    )(*found)
    return (new_embed, new_state.reshape(16), dest, rel_grad.reshape(512, 256))


def solution(mesh):
    return jax.shard_map(
        on_device,
        mesh=mesh,
        in_specs=(
            P("blk", None),
            P("blk"),
            P(),
            P("blk", "grp", None, None, None),
            P("blk", "grp", None, None, None),
            P("blk", "grp", None, None, None),
            P("blk", "grp", None, None, None),
            P("blk", "grp", None),
        ),
        out_specs=(P(("blk", "grp"), None), P(("blk", "grp")), P(("blk", "grp"), None), P()),
        check_vma=False,
    )
```

time: 69.3 us -> 65.1 us (0.939)
  Pallas kernels: 68.4 us -> 64.3 us
    pallas_call x2 -> x1, Pallas kernels: 67.6 us -> 63.4 us  [on_device(): pl.pallas_call(window_kernel, out_shape=results, in_specs=[hbm] * 8, out_...]
where the time goes in v4:
time: 65.1 us; the launch traced here: 64.9 us
  Pallas kernels  64.3 us (99%)
    pallas_call x1, Pallas kernels, on_device(): pl.pallas_call(window_kernel, out_shape=results, in_specs=[hbm] * 8, out_...  63.4 us

profile of v4, /device:TPU:1, one launch (start us, length us, event | category | flops | bytes accessed | tf_op | source)
XLA Modules:
  0.0 64.9 jit_solution(8595753875452864537)
XLA Ops:
  0.6 63.4 %window.1 = (f32[16,256]{1,0:T(8,128)S(1)}, f32[1,16]{1,0:T(1,128)S(1)}, f32[16,256]{1,0:T(8,128)S(1)}, f32[2,32,8,256]{3,2,1,0:T(8,128)S(1)}) custom-call(bf16[256,256]{1,0:T(8,128)(2,1)} %embed.1, f32[512,256]{1,0:T(8,128)} %relation.1, s32[1,1,4,2,128]{4,3,2,1,0:T(2,128)} %src.1, s32[1,1,4,2,128]{4,3,2,1,0:T(2,128)} %dst.1, s32[1,1,4,2,128]{4,3,2,1,0:T(2,128)} %rel.1, ...), custom_call_target="tpu_custom_call" | custom-call | tf_op jit(solution)/shard_map/window/pallas_call | solution.py:442
  64.1 0.8 %finish.1 = (f32[16,256]{1,0:T(8,128)}, f32[1,16]{1,0:T(1,128)}, f32[16,256]{1,0:T(8,128)}, f32[2,32,8,256]{3,2,1,0:T(8,128)}) custom-call(f32[16,256]{1,0:T(8,128)S(1)} %get-tuple-element.12.a, f32[1,16]{1,0:T(1,128)S(1)} %get-tuple-element.13.b, f32[16,256]{1,0:T(8,128)S(1)} %get-tuple-element.14.c, f32[2,32,8,256]{3,2,1,0:T(8,128)S(1)} %get-tuple-element.15.d), custom_call_target="tpu_custom_call" | custom-call | tf_op jit(solution)/shard_map/finish/pallas_call | solution.py:497

commit v5 on v4

--- a/solution.py
+++ b/solution.py
@@ -28,6 +28,10 @@
     return (lax.rem(y, 4) * NZ + z, lax.div(y, 4) * 8 + x * 2 + c)
 
 
+def pairing(z, x):
+    return x + lax.rem(z, 2) * (3 - 2 * x)
+
+
 def remote(src, dst, send, recv, where):
     return pltpu.make_async_remote_copy(
         src_ref=src, dst_ref=dst, send_sem=send, recv_sem=recv, device_id=where, device_id_type=MESH
@@ -55,38 +59,54 @@
     return jnp.concatenate([rows[0:1], rows[1:2]], axis=1)
 
 
-def bucket_gradients(index, slab, src_rows, rel_rows, g_src, g_dst, g_rel):
-    def split(ref, rows, value):
-        top = value.astype(BF16)
-        ref[rows, 0:256] = top
-        ref[rows, 256:512] = (value - top.astype(F32)).astype(BF16)
-
-    lane = lax.broadcasted_iota(jnp.int32, (256, 256), 1)
-    for k, d in enumerate((0, 1, 3, 2)):
+def split(ref, rows, value):
+    top = value.astype(BF16)
+    ref[rows, 0:256] = top
+    ref[rows, 256:512] = (value - top.astype(F32)).astype(BF16)
+
+
+def edge_gradients(slab, src_rows, rel_rows, pick_dst, pick_neg, scaled_grad, pos_grad, weight, g_rel):
+    for k in range(NX):
         edges = slice(k * 256, k * 256 + 256)
-        negs = slice(1024 + k * 256, 1024 + k * 256 + 256)
         src_v = src_rows[edges]
-        rel_v = rel_rows[edges]
-        dst_v = dot(hot(lane == columns_of(index[d, 1])), slab[...])
-        neg_v = dot(hot(lane == columns_of(index[d, 3])), slab[...]).astype(BF16)
-        scaled = src_v * rel_v
+        scaled = src_v * rel_rows[edges]
+        dst_v = dot(pick_dst[edges], slab[...])
+        neg_v = dot(pick_neg[edges], slab[...]).astype(BF16)
         positive = jnp.sum(scaled * dst_v, axis=1, keepdims=True)
-        pos_grad = -jax.nn.sigmoid(-positive)
+        pull = -jax.nn.sigmoid(-positive)
+        pos_grad[edges] = pull
         scaled_b = scaled.astype(BF16)
         from_neg = []
-        neg_g = []
         for j in range(2):
             block = slice(j * 128, j * 128 + 128)
             s, n = scaled_b[block], neg_v[block]
             score = lax.dot_general(s, n, (((1,), (1,)), ((), ())), preferred_element_type=F32)
-            weight = (jax.nn.sigmoid(score) * (1.0 / 128.0)).astype(BF16)
-            from_neg.append(dot(weight, n))
-            neg_g.append(lax.dot_general(weight, s, (((0,), (0,)), ((), ())), preferred_element_type=F32))
-        scaled_grad = pos_grad * dst_v + jnp.concatenate(from_neg, axis=0)
-        split(g_rel, edges, scaled_grad * src_v)
-        split(g_src, edges, scaled_grad * rel_v)
-        split(g_dst, edges, pos_grad * scaled)
-        split(g_dst, negs, jnp.concatenate(neg_g, axis=0))
+            push = (jax.nn.sigmoid(score) * (1.0 / 128.0)).astype(BF16)
+            weight[k * 256 + j * 128 : k * 256 + j * 128 + 128] = push
+            from_neg.append(dot(push, n))
+        grad = pull * dst_v + jnp.concatenate(from_neg, axis=0)
+        scaled_grad[edges] = grad
+        split(g_rel, edges, grad * src_v)
+
+
+def dst_gradients(src_rows, rel_rows, pos_grad, weight, g_dst):
+    for k in range(NX):
+        edges = slice(k * 256, k * 256 + 256)
+        scaled = src_rows[edges] * rel_rows[edges]
+        scaled_b = scaled.astype(BF16)
+        split(g_dst, edges, pos_grad[edges] * scaled)
+        for j in range(2):
+            push = weight[k * 256 + j * 128 : k * 256 + j * 128 + 128]
+            value = lax.dot_general(
+                push, scaled_b[j * 128 : j * 128 + 128], (((0,), (0,)), ((), ())), preferred_element_type=F32
+            )
+            split(g_dst, slice(1024 + k * 256 + j * 128, 1024 + k * 256 + j * 128 + 128), value)
+
+
+def src_gradients(rel_rows, scaled_grad, g_src):
+    for k in range(NX):
+        edges = slice(k * 256, k * 256 + 256)
+        split(g_src, edges, scaled_grad[edges] * rel_rows[edges])
 
 
 def both_terms(h, g):
@@ -123,6 +143,11 @@
     g_src,
     g_dst,
     g_rel,
+    pick_dst,
+    pick_neg,
+    scaled_grad,
+    pos_grad,
+    weight,
     own_state,
     rel_far,
     rel_near,
@@ -164,11 +189,12 @@
     load_state.start()
 
     sibling = (b, g + 1 - 2 * c)
-    ahead = (lax.rem(b + x, NB), g)
-    behind = (lax.rem(b + NB - x, NB), g)
+    turn = pairing(z, x)
+    behind = (lax.rem(b + NB - turn, NB), g)
+    wanted = [(s, pairing(z + s, x) == s, (lax.rem(b + s, NB), g)) for s in (3, 2, 1)]
     opposite = at(z, lax.rem(y + 4, NY), x, c)
     yh = lax.div(y, 4)
-    base = lax.rem(b + 3 + NB - x, NB)
+    base = lax.rem(b + 3 + NB - turn, NB)
     row_of = lax.div(g, 8) * 8 + c
     mine = x * NY + y
 
@@ -199,7 +225,7 @@
         greet(along_y(d))
         greet(along_z(d))
 
-    @pl.when(x > 0)
+    @pl.when(turn > 0)
     def _():
         greet(behind)
 
@@ -213,25 +239,27 @@
         for i in range(1, 4):
             packed[t, i] = loaded[i, t]
     load_own.wait()
-    pl.semaphore_wait(pltpu.get_barrier_semaphore(), jnp.where(x > 0, 9, 8))
+    pl.semaphore_wait(pltpu.get_barrier_semaphore(), 8 + sum(jnp.where(asked, 1, 0) for _, asked, _ in wanted))
 
     half = pl.ds(pl.multiple_of(c * 128, 128), 128)
     other = pl.ds(pl.multiple_of((1 - c) * 128, 128), 128)
 
-    @pl.when(x > 0)
-    def _():
-        remote(own.at[half], slab.at[half], slab_send.at[0], slab_recv.at[0], ahead).start()
+    for s, asked, ahead in wanted:
+
+        @pl.when(asked)
+        def _():
+            remote(own.at[half], slab.at[half], slab_send.at[s], slab_recv.at[0], ahead).start()
 
     sends = {}
     for d in (2, 1, 3):
         there = lax.rem(x + d, NX)
-        sends[d] = remote(packed.at[there], index.at[d], idx_send.at[d - 1], idx_recv.at[d - 1], along_x(d))
+        sends[d] = remote(packed.at[pairing(z, there)], index.at[d], idx_send.at[d - 1], idx_recv.at[d - 1], along_x(d))
         sends[d].start()
     tell(0, along_y(1), along_y(-1))
     tell(1, along_z(1), along_z(-1))
-    index[0:1] = packed[pl.ds(x, 1)]
-
-    @pl.when(x == 0)
+    index[0:1] = packed[pl.ds(turn, 1)]
+
+    @pl.when(turn == 0)
     def _():
         slab[...] = own[...]
 
@@ -263,35 +291,29 @@
             tell(5, along_z(4), along_z(-4))
         if k == 3:
             pl.semaphore_wait(here.at[4], 3)
-
-            @pl.when(x < 3)
-            def _():
-                tell(6, along_z(x - 3))
+            tell(6, along_z(-1), along_z(-2), along_z(-3))
 
         if d > 0:
             sends[d].wait_recv()
         src_rows[edges] = dot(hot(lane == columns_of(index[d, 0])), own[...])
         pieces = dot(hot(lane_r == columns_of(index[d, 2])), parts[...])
         rel_rows[edges] = (pieces[:, 0:256] + pieces[:, 256:512]) + pieces[:, 512:768]
+        pick_dst[edges] = hot(lane == columns_of(index[d, 1]))
+        pick_neg[edges] = hot(lane == columns_of(index[d, 3]))
         hot_src[:, edges] = hot(sub == line_of(index[d, 0]))
         hot_dst[:, edges] = hot(sub == line_of(index[d, 1]))
         hot_dst[:, negs] = hot(sub == line_of(index[d, 3]))
         hot_rel[:, :, edges] = hot(sub_r == line_of(index[d, 2])[None])
 
-    @pl.when(x > 0)
+    @pl.when(turn > 0)
     def _():
-        first = remote(own.at[half], slab.at[half], slab_send.at[0], slab_recv.at[0], ahead)
-        second = remote(slab.at[half], slab.at[half], slab_send.at[1], slab_recv.at[1], sibling)
-        first.wait_recv()
+        second = remote(slab.at[half], slab.at[half], slab_send.at[0], slab_recv.at[1], sibling)
+        remote(own.at[half], slab.at[half], slab_send.at[0], slab_recv.at[0], sibling).wait_recv()
         second.start()
-        first.wait_send()
+        remote(slab.at[other], slab.at[other], slab_send.at[0], slab_recv.at[1], sibling).wait_recv()
         second.wait_send()
-        remote(slab.at[other], slab.at[other], slab_send.at[1], slab_recv.at[1], sibling).wait_recv()
-
-    for d in (1, 2, 3):
-        sends[d].wait_send()
-
-    bucket_gradients(index, slab, src_rows, rel_rows, g_src, g_dst, g_rel)
+
+    edge_gradients(slab, src_rows, rel_rows, pick_dst, pick_neg, scaled_grad, pos_grad, weight, g_rel)
     rel_far[...] = both_terms(hot_rel[pl.ds(1 - c, 1)][0], g_rel[...]).reshape(32, 8, 256)
 
     def pair(source, target, i):
@@ -303,10 +325,10 @@
     rel_c = {}
     for dx in (2, 1, 3, 0):
         rows = pl.ds(lax.rem(x + dx, NX) * NY, NY)
-        mirror = pl.ds(lax.rem(x + dx, NX) * NY, NY)
-        rel_c[dx] = remote(rel_far.at[rows], rel_pair.at[mirror], send.at[0], pair_recv.at[dx], sibling)
+        rel_c[dx] = remote(rel_far.at[rows], rel_pair.at[rows], send.at[0], pair_recv.at[dx], sibling)
         rel_c[dx].start()
     rel_near[...] = both_terms(hot_rel[pl.ds(c, 1)][0], g_rel[...]).reshape(32, 8, 256)
+    dst_gradients(src_rows, rel_rows, pos_grad, weight, g_dst)
     for dx in (2, 1, 3, 0):
         rows = pl.ds(lax.rem(x + dx, NX) * NY, NY)
         rel_c[dx].wait_recv()
@@ -318,23 +340,21 @@
 
     dst_part[...] = both_terms(hot_dst[...], g_dst[...]).reshape(2, 4, 2, 16, 256)
     dst_c.start()
+    src_gradients(rel_rows, scaled_grad, g_src)
     src_part[...] = both_terms(hot_src[...], g_src[...]).reshape(2, 4, 2, 16, 256)
     dst_c.wait_recv()
     dst_pair[...] = dst_pair[...] + dst_part[:, :, pl.ds(c, 1)].reshape(2, 4, 16, 256)
-    @pl.when(x < 3)
+    pl.semaphore_wait(here.at[6], 3)
+    for px in range(NX):
+        to = (base, row_of + 2 * px)
+
+        @pl.when(jnp.logical_or(turn != 3, x != px))
+        def _():
+            remote(dst_pair.at[:, px], dst_x.at[turn], dst_send.at[px], dst_recv.at[turn], to).start()
+
+    @pl.when(turn == 3)
     def _():
-        pl.semaphore_wait(here.at[6], 1)
-
-    for t in range(NX):
-        to = (base, row_of + 2 * t)
-
-        @pl.when(jnp.logical_or(x != 3, t != 3))
-        def _():
-            remote(dst_pair.at[:, t], dst_x.at[x], dst_send.at[t], dst_recv.at[x], to).start()
-
-    @pl.when(x == 3)
-    def _():
-        dst_x[3] = dst_pair[:, 3]
+        dst_x[3:4] = dst_pair[:, pl.ds(x, 1)].reshape(1, 2, 16, 256)
 
     src_c.start()
 
@@ -364,11 +384,10 @@
     src_far = remote(src_half.at[1 - yh], src_y, send.at[9], recv.at[9], opposite)
     src_far.start()
     for t in range(NX):
-        source = (lax.rem(b + NB - 3 + t, NB), row_of + 2 * t)
-
-        @pl.when(jnp.logical_or(x != 3, t != 3))
+
+        @pl.when(jnp.logical_or(turn != 3, t != 3))
         def _():
-            remote(dst_pair.at[:, t], dst_x.at[t], dst_send.at[t], dst_recv.at[t], source).wait_recv()
+            remote(dst_pair.at[:, t], dst_x.at[t], dst_send.at[t], dst_recv.at[t], sibling).wait_recv()
 
     dst_x[0] = (dst_x[0] + dst_x[1]) + (dst_x[2] + dst_x[3])
     dst_far = remote(dst_x.at[0, 1 - yh], dst_y, send.at[10], recv.at[10], opposite)
@@ -395,6 +414,14 @@
         remote(rel_out.at[c, group], rel_out.at[c, group], send.at[12], recv.at[12], sibling).start()
     dst_far.wait_recv()
     dest_out[...] = dst_x[0, pl.ds(yh, 1)].reshape(16, 256) + dst_y[...]
+    for d in (1, 2, 3):
+        sends[d].wait_send()
+    for s, asked, ahead in wanted:
+
+        @pl.when(asked)
+        def _():
+            remote(own.at[half], slab.at[half], slab_send.at[s], slab_recv.at[0], ahead).wait_send()
+
     remote(rel_far, rel_pair, send.at[0], recv.at[0], sibling).wait_send()
     src_c.wait_send()
     dst_c.wait_send()
@@ -403,11 +430,11 @@
     chunks(rel_xy, 31, send.at[11]).wait()
     for copy in src_sends:
         copy.wait_send()
-    for t in range(NX):
-
-        @pl.when(jnp.logical_or(x != 3, t != 3))
+    for px in range(NX):
+
+        @pl.when(jnp.logical_or(turn != 3, x != px))
         def _():
-            remote(dst_pair.at[:, t], dst_x.at[x], dst_send.at[t], dst_recv.at[x], sibling).wait_send()
+            remote(dst_pair.at[:, px], dst_x.at[0], dst_send.at[px], dst_recv.at[0], sibling).wait_send()
 
     src_far.wait_send()
     dst_far.wait_send()
@@ -461,6 +488,11 @@
             held((1024, 512), BF16),
             held((2048, 512), BF16),
             held((1024, 512), BF16),
+            held((1024, 256), BF16),
+            held((1024, 256), BF16),
+            held((1024, 256)),
+            held((1024, 1)),
+            held((1024, 128), BF16),
             held((1, 256)),
             held((32, 8, 256)),
             held((32, 8, 256)),
@@ -479,7 +511,7 @@
             dma((8,)),
             dma((3,)),
             dma((3,)),
-            dma((2,)),
+            dma((4,)),
             dma((2,)),
             dma((13,)),
             dma((13,)),

time: 65.1 us -> 63.5 us (0.975)
  Pallas kernels: 64.3 us -> 62.7 us
    pallas_call x1, Pallas kernels: 63.4 us -> 61.8 us  [on_device(): pl.pallas_call(window_kernel, out_shape=results, in_specs=[hbm] * 8, out_...]
where the time goes in v5:
time: 63.5 us; the launch traced here: 63.3 us
  Pallas kernels  62.7 us (99%)
  between operations  0.64 us (1%)
    pallas_call x1, Pallas kernels, on_device(): pl.pallas_call(window_kernel, out_shape=results, in_specs=[hbm] * 8, out_...  61.8 us

profile of v5, /device:TPU:1, one launch (start us, length us, event | category | flops | bytes accessed | tf_op | source)
XLA Modules:
  0.0 63.3 jit_solution(13212930770968617379)
XLA Ops:
  0.6 61.8 %window.1 = (f32[16,256]{1,0:T(8,128)S(1)}, f32[1,16]{1,0:T(1,128)S(1)}, f32[16,256]{1,0:T(8,128)S(1)}, f32[2,32,8,256]{3,2,1,0:T(8,128)S(1)}) custom-call(bf16[256,256]{1,0:T(8,128)(2,1)} %embed.1, f32[512,256]{1,0:T(8,128)} %relation.1, s32[1,1,4,2,128]{4,3,2,1,0:T(2,128)} %src.1, s32[1,1,4,2,128]{4,3,2,1,0:T(2,128)} %dst.1, s32[1,1,4,2,128]{4,3,2,1,0:T(2,128)} %rel.1, ...), custom_call_target="tpu_custom_call" | custom-call | tf_op jit(solution)/shard_map/window/pallas_call | solution.py:469
  62.5 0.8 %finish.1 = (f32[16,256]{1,0:T(8,128)}, f32[1,16]{1,0:T(1,128)}, f32[16,256]{1,0:T(8,128)}, f32[2,32,8,256]{3,2,1,0:T(8,128)}) custom-call(f32[16,256]{1,0:T(8,128)S(1)} %get-tuple-element.12.a, f32[1,16]{1,0:T(1,128)S(1)} %get-tuple-element.13.b, f32[16,256]{1,0:T(8,128)S(1)} %get-tuple-element.14.c, f32[2,32,8,256]{3,2,1,0:T(8,128)S(1)} %get-tuple-element.15.d), custom_call_target="tpu_custom_call" | custom-call | tf_op jit(solution)/shard_map/finish/pallas_call | solution.py:529

commit v6 on v5

--- a/solution.py
+++ b/solution.py
@@ -63,6 +63,14 @@
     top = value.astype(BF16)
     ref[rows, 0:256] = top
     ref[rows, 256:512] = (value - top.astype(F32)).astype(BF16)
+
+
+def split_halves(ref, rows, value):
+    top = value.astype(BF16)
+    low = (value - top.astype(F32)).astype(BF16)
+    for h in range(2):
+        ref[rows, 256 * h : 256 * h + 128] = top[:, 128 * h : 128 * h + 128]
+        ref[rows, 256 * h + 128 : 256 * h + 256] = low[:, 128 * h : 128 * h + 128]
 
 
 def edge_gradients(slab, src_rows, rel_rows, pick_dst, pick_neg, scaled_grad, pos_grad, weight, g_rel):
@@ -86,7 +94,7 @@
             from_neg.append(dot(push, n))
         grad = pull * dst_v + jnp.concatenate(from_neg, axis=0)
         scaled_grad[edges] = grad
-        split(g_rel, edges, grad * src_v)
+        split_halves(g_rel, edges, grad * src_v)
 
 
 def dst_gradients(src_rows, rel_rows, pos_grad, weight, g_dst):
@@ -161,6 +169,7 @@
     src_x,
     dst_x,
     src_half,
+    dst_half,
     src_y,
     dst_y,
     load_sem,
@@ -173,6 +182,8 @@
     dst_send,
     dst_recv,
     pair_recv,
+    xy_recv,
+    z_recv,
     all_recv,
     here,
 ):
@@ -314,61 +325,55 @@
         second.wait_send()
 
     edge_gradients(slab, src_rows, rel_rows, pick_dst, pick_neg, scaled_grad, pos_grad, weight, g_rel)
-    rel_far[...] = both_terms(hot_rel[pl.ds(1 - c, 1)][0], g_rel[...]).reshape(32, 8, 256)
-
     def pair(source, target, i):
         return remote(source, target, send.at[i], recv.at[i], sibling)
 
+    def chunks(n, sem):
+        return pltpu.make_async_copy(rel_xy.at[0, pl.ds(0, n)], rel_xy.at[0, pl.ds(0, n)], sem)
+
+    def half_terms(core, h):
+        both = dot(hot_rel[pl.ds(core, 1)][0], g_rel[:, 256 * h : 256 * h + 256])
+        return (both[:, 0:128] + both[:, 128:256]).reshape(32, 8, 128)
+
     src_c = pair(src_part.at[:, :, 1 - c], src_pair, 1)
     dst_c = pair(dst_part.at[:, :, 1 - c], dst_pair, 2)
-
-    rel_c = {}
-    for dx in (2, 1, 3, 0):
-        rows = pl.ds(lax.rem(x + dx, NX) * NY, NY)
-        rel_c[dx] = remote(rel_far.at[rows], rel_pair.at[rows], send.at[0], pair_recv.at[dx], sibling)
-        rel_c[dx].start()
-    rel_near[...] = both_terms(hot_rel[pl.ds(c, 1)][0], g_rel[...]).reshape(32, 8, 256)
+    offsets = [(dx, dy) for dx in (2, 1, 3, 0) for dy in y_order if (dx, dy) != (0, 0)]
+
+    rel_c = [remote(rel_far.at[h], rel_pair.at[h], send.at[0], pair_recv.at[h], sibling) for h in range(2)]
+    for h in range(2):
+        rel_far[h] = half_terms(1 - c, h)
+        rel_c[h].start()
+    for h in range(2):
+        rel_near[h] = half_terms(c, h)
+    rel_c[0].wait_recv()
+    rel_near[0] = rel_near[0] + rel_pair[0]
+    for i, (dx, dy) in enumerate(offsets):
+        chunk, where = plane(dx, dy)
+        remote(rel_near.at[0, chunk], rel_xy.at[0, i], send.at[3], xy_recv.at[0], where).start()
     dst_gradients(src_rows, rel_rows, pos_grad, weight, g_dst)
-    for dx in (2, 1, 3, 0):
-        rows = pl.ds(lax.rem(x + dx, NX) * NY, NY)
-        rel_c[dx].wait_recv()
-        rel_near[rows] = rel_near[rows] + rel_pair[rows]
-        for dy in y_order:
-            if (dx, dy) != (0, 0):
-                chunk, where = plane(dx, dy)
-                remote(rel_near.at[chunk], rel_xy.at[(dx * NY + dy) - 1], send.at[3], recv.at[3], where).start()
-
     dst_part[...] = both_terms(hot_dst[...], g_dst[...]).reshape(2, 4, 2, 16, 256)
     dst_c.start()
+    rel_c[1].wait_recv()
+    rel_near[1] = rel_near[1] + rel_pair[1]
+    for i, (dx, dy) in enumerate(offsets):
+        chunk, where = plane(dx, dy)
+        remote(rel_near.at[1, chunk], rel_xy.at[1, i], send.at[3], xy_recv.at[1], where).start()
+
+    dst_c.wait_recv()
+    dst_pair[...] = dst_pair[...] + dst_part[:, :, pl.ds(c, 1)].reshape(2, 4, 16, 256)
+    dst_far = remote(dst_pair.at[1 - yh], dst_y, send.at[10], recv.at[10], opposite)
     src_gradients(rel_rows, scaled_grad, g_src)
     src_part[...] = both_terms(hot_src[...], g_src[...]).reshape(2, 4, 2, 16, 256)
-    dst_c.wait_recv()
-    dst_pair[...] = dst_pair[...] + dst_part[:, :, pl.ds(c, 1)].reshape(2, 4, 16, 256)
-    pl.semaphore_wait(here.at[6], 3)
-    for px in range(NX):
-        to = (base, row_of + 2 * px)
-
-        @pl.when(jnp.logical_or(turn != 3, x != px))
-        def _():
-            remote(dst_pair.at[:, px], dst_x.at[turn], dst_send.at[px], dst_recv.at[turn], to).start()
-
-    @pl.when(turn == 3)
-    def _():
-        dst_x[3:4] = dst_pair[:, pl.ds(x, 1)].reshape(1, 2, 16, 256)
-
     src_c.start()
 
-    offsets = [(dx, dy) for dx in (2, 1, 3, 0) for dy in y_order if (dx, dy) != (0, 0)]
-
-    def chunks(ref, n, sem):
-        return pltpu.make_async_copy(ref.at[pl.ds(0, n)], ref.at[pl.ds(0, n)], sem)
-
-    chunks(rel_xy, 31, recv.at[3]).wait()
-    rel_z[pl.ds(z, 1)] = (rel_near[pl.ds(mine, 1)][0] + jnp.sum(rel_xy[...], axis=0))[None]
     pl.semaphore_wait(here.at[5], 2)
-    for dz in z_offsets:
-        where = along_z(dz)
-        remote(rel_z.at[z], rel_z.at[z], send.at[8], recv.at[8], where).start()
+    for h in range(2):
+        chunks(31, xy_recv.at[h]).wait()
+        rel_z[h, pl.ds(z, 1)] = (rel_near[h, pl.ds(mine, 1)][0] + jnp.sum(rel_xy[h], axis=0))[None]
+        for dz in z_offsets:
+            remote(rel_z.at[h, z], rel_z.at[h, z], send.at[8], z_recv.at[h], along_z(dz)).start()
+        if h == 0:
+            dst_far.start()
 
     src_c.wait_recv()
     src_pair[...] = src_pair[...] + src_part[:, :, pl.ds(c, 1)].reshape(2, 4, 16, 256)
@@ -383,20 +388,30 @@
     src_half[...] = (src_pair[:, pl.ds(x, 1)].reshape(2, 16, 256) + src_x[1]) + (src_x[2] + src_x[3])
     src_far = remote(src_half.at[1 - yh], src_y, send.at[9], recv.at[9], opposite)
     src_far.start()
-    for t in range(NX):
-
-        @pl.when(jnp.logical_or(turn != 3, t != 3))
+
+    dst_far.wait_recv()
+    dst_half[...] = dst_pair[pl.ds(yh, 1)][0] + dst_y[...]
+    pl.semaphore_wait(here.at[6], 3)
+    for px in range(NX):
+        to = (base, row_of + 2 * px)
+
+        @pl.when(jnp.logical_or(turn != 3, x != px))
         def _():
-            remote(dst_pair.at[:, t], dst_x.at[t], dst_send.at[t], dst_recv.at[t], sibling).wait_recv()
-
-    dst_x[0] = (dst_x[0] + dst_x[1]) + (dst_x[2] + dst_x[3])
-    dst_far = remote(dst_x.at[0, 1 - yh], dst_y, send.at[10], recv.at[10], opposite)
-    dst_far.start()
-    chunks(rel_z, 15, recv.at[8]).wait()
-    rel_out[pl.ds(c, 1), pl.ds(mine, 1)] = jnp.sum(rel_z[...], axis=0)[None, None]
-    for dx, dy in offsets:
-        _, where = plane(dx, dy)
-        remote(rel_out.at[c, mine], rel_out.at[c, mine], send.at[11], all_recv.at[dx], where).start()
+            remote(dst_half.at[px], dst_x.at[turn], dst_send.at[px], dst_recv.at[turn], to).start()
+
+    @pl.when(turn == 3)
+    def _():
+        dst_x[3:4] = dst_half[pl.ds(x, 1)]
+
+    for h in range(2):
+        cols = slice(128 * h, 128 * h + 128)
+        chunks(15, z_recv.at[h]).wait()
+        rel_out[pl.ds(c, 1), pl.ds(mine, 1), :, cols] = jnp.sum(rel_z[h], axis=0)[None, None]
+        for dx, dy in offsets:
+            _, where = plane(dx, dy)
+            out = rel_out.at[c, mine, :, cols]
+            remote(out, out, send.at[11], all_recv.at[h, dx], where).start()
+
     load_state.wait()
     src_far.wait_recv()
     total = src_half[pl.ds(yh, 1)][0] + src_y[...]
@@ -408,12 +423,19 @@
     lane16 = lax.broadcasted_iota(jnp.int32, (16, 16), 1)
     line16 = lax.broadcasted_iota(jnp.int32, (16, 16), 0)
     new_state[...] = jnp.sum(jnp.where(lane16 == line16, fresh, 0.0), axis=0, keepdims=True)
-    for dx in (0, 1, 3, 2):
-        chunks(rel_xy, 7 if dx == 0 else 8, all_recv.at[dx]).wait()
-        group = pl.ds(lax.rem(x + NX - dx, NX) * NY, NY)
-        remote(rel_out.at[c, group], rel_out.at[c, group], send.at[12], recv.at[12], sibling).start()
-    dst_far.wait_recv()
-    dest_out[...] = dst_x[0, pl.ds(yh, 1)].reshape(16, 256) + dst_y[...]
+
+    for h in range(2):
+        for dx in (0, 1, 3, 2):
+            chunks(7 if dx == 0 else 8, all_recv.at[h, dx]).wait()
+            group = rel_out.at[c, pl.ds(lax.rem(x + NX - dx, NX) * NY, NY), :, 128 * h : 128 * h + 128]
+            remote(group, group, send.at[12], recv.at[12], sibling).start()
+    for t in range(NX):
+
+        @pl.when(jnp.logical_or(turn != 3, t != 3))
+        def _():
+            remote(dst_half.at[t], dst_x.at[t], dst_send.at[t], dst_recv.at[t], sibling).wait_recv()
+
+    dest_out[...] = (dst_x[0] + dst_x[1]) + (dst_x[2] + dst_x[3])
     for d in (1, 2, 3):
         sends[d].wait_send()
     for s, asked, ahead in wanted:
@@ -425,16 +447,17 @@
     remote(rel_far, rel_pair, send.at[0], recv.at[0], sibling).wait_send()
     src_c.wait_send()
     dst_c.wait_send()
-    chunks(rel_xy, 31, send.at[3]).wait()
-    chunks(rel_z, 15, send.at[8]).wait()
-    chunks(rel_xy, 31, send.at[11]).wait()
+    for _ in range(2):
+        chunks(31, send.at[3]).wait()
+        chunks(15, send.at[8]).wait()
+        chunks(31, send.at[11]).wait()
     for copy in src_sends:
         copy.wait_send()
     for px in range(NX):
 
         @pl.when(jnp.logical_or(turn != 3, x != px))
         def _():
-            remote(dst_pair.at[:, px], dst_x.at[0], dst_send.at[px], dst_recv.at[0], sibling).wait_send()
+            remote(dst_half.at[px], dst_x.at[0], dst_send.at[px], dst_recv.at[0], sibling).wait_send()
 
     src_far.wait_send()
     dst_far.wait_send()
@@ -494,20 +517,21 @@
             held((1024, 1)),
             held((1024, 128), BF16),
             held((1, 256)),
-            held((32, 8, 256)),
-            held((32, 8, 256)),
+            held((2, 32, 8, 128)),
+            held((2, 32, 8, 128)),
             held((2, 4, 2, 16, 256)),
             held((2, 4, 2, 16, 256)),
-            held((32, 8, 256)),
+            held((2, 32, 8, 128)),
             held((2, 4, 16, 256)),
             held((2, 4, 16, 256)),
-            held((31, 8, 256)),
-            held((16, 8, 256)),
+            held((2, 31, 8, 128)),
+            held((2, 16, 8, 128)),
             held((4, 2, 16, 256)),
-            held((4, 2, 16, 256)),
+            held((4, 16, 256)),
             held((2, 16, 256)),
+            held((4, 16, 256)),
             held((16, 256)),
-            held((16, 256)),
+            held((4, 16, 256)),
             dma((8,)),
             dma((3,)),
             dma((3,)),
@@ -517,8 +541,10 @@
             dma((13,)),
             dma((4,)),
             dma((4,)),
-            dma((4,)),
-            dma((4,)),
+            dma((2,)),
+            dma((2,)),
+            dma((2,)),
+            dma((2, 4)),
             pltpu.SemaphoreType.REGULAR((7,)),
         ],
         compiler_params=pltpu.CompilerParams(

time: 63.5 us -> 60.7 us (0.956)
  Pallas kernels: 62.7 us -> 59.9 us
    pallas_call x1, Pallas kernels: 61.8 us -> 59 us  [on_device(): pl.pallas_call(window_kernel, out_shape=results, in_specs=[hbm] * 8, out_...]
where the time goes in v6:
time: 60.7 us; the launch traced here: 60.5 us
  Pallas kernels  59.9 us (99%)
  between operations  0.64 us (1%)
    pallas_call x1, Pallas kernels, on_device(): pl.pallas_call(window_kernel, out_shape=results, in_specs=[hbm] * 8, out_...  59 us

profile of v6, /device:TPU:1, one launch (start us, length us, event | category | flops | bytes accessed | tf_op | source)
XLA Modules:
  0.0 60.5 jit_solution(70535297560055077)
XLA Ops:
  0.6 59.0 %window.1 = (f32[16,256]{1,0:T(8,128)S(1)}, f32[1,16]{1,0:T(1,128)S(1)}, f32[16,256]{1,0:T(8,128)S(1)}, f32[2,32,8,256]{3,2,1,0:T(8,128)S(1)}) custom-call(bf16[256,256]{1,0:T(8,128)(2,1)} %embed.1, f32[512,256]{1,0:T(8,128)} %relation.1, s32[1,1,4,2,128]{4,3,2,1,0:T(2,128)} %src.1, s32[1,1,4,2,128]{4,3,2,1,0:T(2,128)} %dst.1, s32[1,1,4,2,128]{4,3,2,1,0:T(2,128)} %rel.1, ...), custom_call_target="tpu_custom_call" | custom-call | tf_op jit(solution)/shard_map/window/pallas_call | solution.py:492
  59.7 0.8 %finish.1 = (f32[16,256]{1,0:T(8,128)}, f32[1,16]{1,0:T(1,128)}, f32[16,256]{1,0:T(8,128)}, f32[2,32,8,256]{3,2,1,0:T(8,128)}) custom-call(f32[16,256]{1,0:T(8,128)S(1)} %get-tuple-element.12.a, f32[1,16]{1,0:T(1,128)S(1)} %get-tuple-element.13.b, f32[16,256]{1,0:T(8,128)S(1)} %get-tuple-element.14.c, f32[2,32,8,256]{3,2,1,0:T(8,128)S(1)} %get-tuple-element.15.d), custom_call_target="tpu_custom_call" | custom-call | tf_op jit(solution)/shard_map/finish/pallas_call | solution.py:555

commit v7 on v6

--- a/solution.py
+++ b/solution.py
@@ -185,6 +185,8 @@
     xy_recv,
     z_recv,
     all_recv,
+    far_send,
+    far_recv,
     here,
 ):
     b, g, z, y, x, c = position()
@@ -205,8 +207,6 @@
     wanted = [(s, pairing(z + s, x) == s, (lax.rem(b + s, NB), g)) for s in (3, 2, 1)]
     opposite = at(z, lax.rem(y + 4, NY), x, c)
     yh = lax.div(y, 4)
-    base = lax.rem(b + 3 + NB - turn, NB)
-    row_of = lax.div(g, 8) * 8 + c
     mine = x * NY + y
 
     y_order = (4, 3, 5, 2, 6, 1, 7, 0)
@@ -361,7 +361,16 @@
 
     dst_c.wait_recv()
     dst_pair[...] = dst_pair[...] + dst_part[:, :, pl.ds(c, 1)].reshape(2, 4, 16, 256)
-    dst_far = remote(dst_pair.at[1 - yh], dst_y, send.at[10], recv.at[10], opposite)
+
+    past = z + 3 - turn >= NZ
+    stays = jnp.logical_not(past)
+    step_lo = lax.rem(lax.rem(y, 4) + 1, 4)
+    to_rows = [remote(dst_pair.at[i], dst_y.at[yh], far_send.at[i], far_recv.at[yh], at(z, i * 4 + step_lo, x, c)) for i in range(2)]
+    to_opposite = remote(dst_pair.at[1 - yh], dst_y.at[yh], far_send.at[0], far_recv.at[yh], opposite)
+
+    def arrived(i):
+        remote(dst_pair.at[0], dst_y.at[i], far_send.at[0], far_recv.at[i], opposite).wait_recv()
+
     src_gradients(rel_rows, scaled_grad, g_src)
     src_part[...] = both_terms(hot_src[...], g_src[...]).reshape(2, 4, 2, 16, 256)
     src_c.start()
@@ -370,10 +379,19 @@
     for h in range(2):
         chunks(31, xy_recv.at[h]).wait()
         rel_z[h, pl.ds(z, 1)] = (rel_near[h, pl.ds(mine, 1)][0] + jnp.sum(rel_xy[h], axis=0))[None]
+        if h == 0:
+
+            @pl.when(past)
+            def _():
+                to_rows[0].start()
+                to_rows[1].start()
+
+            @pl.when(stays)
+            def _():
+                to_opposite.start()
+
         for dz in z_offsets:
             remote(rel_z.at[h, z], rel_z.at[h, z], send.at[8], z_recv.at[h], along_z(dz)).start()
-        if h == 0:
-            dst_far.start()
 
     src_c.wait_recv()
     src_pair[...] = src_pair[...] + src_part[:, :, pl.ds(c, 1)].reshape(2, 4, 16, 256)
@@ -383,25 +401,35 @@
         copy = remote(src_pair.at[:, px], src_x.at[d], send.at[4 + d], recv.at[4 + d], at(z, y, px, c))
         copy.start()
         src_sends.append(copy)
+
+    @pl.when(past)
+    def _():
+        arrived(0)
+        arrived(1)
+        dst_half[...] = dst_y[0] + dst_y[1]
+
+    @pl.when(stays)
+    def _():
+        arrived(1 - yh)
+        dst_half[...] = dst_pair[pl.ds(yh, 1)][0] + dst_y[pl.ds(1 - yh, 1)][0]
+
+    pl.semaphore_wait(here.at[6], 3)
+    for px in range(NX):
+        to = at(lax.rem(z + 3 - turn, NZ), y, px, c)
+
+        @pl.when(jnp.logical_or(turn != 3, x != px))
+        def _():
+            remote(dst_half.at[px], dst_x.at[turn], dst_send.at[px], dst_recv.at[turn], to).start()
+
+    @pl.when(turn == 3)
+    def _():
+        dst_x[3:4] = dst_half[pl.ds(x, 1)]
+
     for copy in src_sends:
         copy.wait_recv()
     src_half[...] = (src_pair[:, pl.ds(x, 1)].reshape(2, 16, 256) + src_x[1]) + (src_x[2] + src_x[3])
     src_far = remote(src_half.at[1 - yh], src_y, send.at[9], recv.at[9], opposite)
     src_far.start()
-
-    dst_far.wait_recv()
-    dst_half[...] = dst_pair[pl.ds(yh, 1)][0] + dst_y[...]
-    pl.semaphore_wait(here.at[6], 3)
-    for px in range(NX):
-        to = (base, row_of + 2 * px)
-
-        @pl.when(jnp.logical_or(turn != 3, x != px))
-        def _():
-            remote(dst_half.at[px], dst_x.at[turn], dst_send.at[px], dst_recv.at[turn], to).start()
-
-    @pl.when(turn == 3)
-    def _():
-        dst_x[3:4] = dst_half[pl.ds(x, 1)]
 
     for h in range(2):
         cols = slice(128 * h, 128 * h + 128)
@@ -460,7 +488,16 @@
             remote(dst_half.at[px], dst_x.at[0], dst_send.at[px], dst_recv.at[0], sibling).wait_send()
 
     src_far.wait_send()
-    dst_far.wait_send()
+
+    @pl.when(past)
+    def _():
+        to_rows[0].wait_send()
+        to_rows[1].wait_send()
+
+    @pl.when(stays)
+    def _():
+        to_opposite.wait_send()
+
     last = remote(rel_out.at[c], rel_out.at[c], send.at[12], recv.at[12], sibling)
     last.wait_send()
     remote(rel_out.at[1 - c], rel_out.at[1 - c], send.at[12], recv.at[12], sibling).wait_recv()
@@ -531,7 +568,7 @@
             held((2, 16, 256)),
             held((4, 16, 256)),
             held((16, 256)),
-            held((4, 16, 256)),
+            held((2, 4, 16, 256)),
             dma((8,)),
             dma((3,)),
             dma((3,)),
@@ -545,6 +582,8 @@
             dma((2,)),
             dma((2,)),
             dma((2, 4)),
+            dma((2,)),
+            dma((2,)),
             pltpu.SemaphoreType.REGULAR((7,)),
         ],
         compiler_params=pltpu.CompilerParams(

time: 60.7 us -> 58.3 us (0.960)
  Pallas kernels: 59.9 us -> 57.5 us
    pallas_call x1, Pallas kernels: 59 us -> 56.7 us  [on_device(): pl.pallas_call(window_kernel, out_shape=results, in_specs=[hbm] * 8, out_...]
where the time goes in v7:
time: 58.3 us; the launch traced here: 58.2 us
  Pallas kernels  57.5 us (99%)
  between operations  0.64 us (1%)
    pallas_call x1, Pallas kernels, on_device(): pl.pallas_call(window_kernel, out_shape=results, in_specs=[hbm] * 8, out_...  56.7 us

profile of v7, /device:TPU:1, one launch (start us, length us, event | category | flops | bytes accessed | tf_op | source)
XLA Modules:
  0.0 58.2 jit_solution(9921330184220354624)
XLA Ops:
  0.6 56.7 %window.1 = (f32[16,256]{1,0:T(8,128)S(1)}, f32[1,16]{1,0:T(1,128)S(1)}, f32[16,256]{1,0:T(8,128)S(1)}, f32[2,32,8,256]{3,2,1,0:T(8,128)S(1)}) custom-call(bf16[256,256]{1,0:T(8,128)(2,1)} %embed.1, f32[512,256]{1,0:T(8,128)} %relation.1, s32[1,1,4,2,128]{4,3,2,1,0:T(2,128)} %src.1, s32[1,1,4,2,128]{4,3,2,1,0:T(2,128)} %dst.1, s32[1,1,4,2,128]{4,3,2,1,0:T(2,128)} %rel.1, ...), custom_call_target="tpu_custom_call" | custom-call | tf_op jit(solution)/shard_map/window/pallas_call | solution.py:529
  57.3 0.8 %finish.1 = (f32[16,256]{1,0:T(8,128)}, f32[1,16]{1,0:T(1,128)}, f32[16,256]{1,0:T(8,128)}, f32[2,32,8,256]{3,2,1,0:T(8,128)}) custom-call(f32[16,256]{1,0:T(8,128)S(1)} %get-tuple-element.12.a, f32[1,16]{1,0:T(1,128)S(1)} %get-tuple-element.13.b, f32[16,256]{1,0:T(8,128)S(1)} %get-tuple-element.14.c, f32[2,32,8,256]{3,2,1,0:T(8,128)S(1)} %get-tuple-element.15.d), custom_call_target="tpu_custom_call" | custom-call | tf_op jit(solution)/shard_map/finish/pallas_call | solution.py:594

commit v8 on v7

--- a/solution.py
+++ b/solution.py
@@ -195,11 +195,6 @@
     load_own = pltpu.make_async_copy(embed, own, load_sem.at[5])
     load_table = pltpu.make_async_copy(relation, table, load_sem.at[6])
     load_state = pltpu.make_async_copy(state, own_state, load_sem.at[7])
-    for copy in loads:
-        copy.start()
-    load_own.start()
-    load_table.start()
-    load_state.start()
 
     sibling = (b, g + 1 - 2 * c)
     turn = pairing(z, x)
@@ -239,6 +234,12 @@
     @pl.when(turn > 0)
     def _():
         greet(behind)
+
+    for copy in loads:
+        copy.start()
+    load_own.start()
+    load_table.start()
+    load_state.start()
 
     for copy in loads:
         copy.wait()
@@ -343,8 +344,7 @@
     for h in range(2):
         rel_far[h] = half_terms(1 - c, h)
         rel_c[h].start()
-    for h in range(2):
-        rel_near[h] = half_terms(c, h)
+    rel_near[0] = half_terms(c, 0)
     rel_c[0].wait_recv()
     rel_near[0] = rel_near[0] + rel_pair[0]
     for i, (dx, dy) in enumerate(offsets):
@@ -353,6 +353,7 @@
     dst_gradients(src_rows, rel_rows, pos_grad, weight, g_dst)
     dst_part[...] = both_terms(hot_dst[...], g_dst[...]).reshape(2, 4, 2, 16, 256)
     dst_c.start()
+    rel_near[1] = half_terms(c, 1)
     rel_c[1].wait_recv()
     rel_near[1] = rel_near[1] + rel_pair[1]
     for i, (dx, dy) in enumerate(offsets):

time: 58.3 us -> 58.2 us (level)
  no operation moved by 1% of the time
where the time goes in v8:
time: 58.2 us; the launch traced here: 58 us
  Pallas kernels  57.4 us (99%)
  between operations  0.64 us (1%)
    pallas_call x1, Pallas kernels, on_device(): pl.pallas_call(window_kernel, out_shape=results, in_specs=[hbm] * 8, out_...  56.6 us

profile of v8, /device:TPU:1, one launch (start us, length us, event | category | flops | bytes accessed | tf_op | source)
XLA Modules:
  0.0 58.0 jit_solution(13031024375368280184)
XLA Ops:
  0.6 56.6 %window.1 = (f32[16,256]{1,0:T(8,128)S(1)}, f32[1,16]{1,0:T(1,128)S(1)}, f32[16,256]{1,0:T(8,128)S(1)}, f32[2,32,8,256]{3,2,1,0:T(8,128)S(1)}) custom-call(bf16[256,256]{1,0:T(8,128)(2,1)} %embed.1, f32[512,256]{1,0:T(8,128)} %relation.1, s32[1,1,4,2,128]{4,3,2,1,0:T(2,128)} %src.1, s32[1,1,4,2,128]{4,3,2,1,0:T(2,128)} %dst.1, s32[1,1,4,2,128]{4,3,2,1,0:T(2,128)} %rel.1, ...), custom_call_target="tpu_custom_call" | custom-call | tf_op jit(solution)/shard_map/window/pallas_call | solution.py:530
  57.2 0.8 %finish.1 = (f32[16,256]{1,0:T(8,128)}, f32[1,16]{1,0:T(1,128)}, f32[16,256]{1,0:T(8,128)}, f32[2,32,8,256]{3,2,1,0:T(8,128)}) custom-call(f32[16,256]{1,0:T(8,128)S(1)} %get-tuple-element.12.a, f32[1,16]{1,0:T(1,128)S(1)} %get-tuple-element.13.b, f32[16,256]{1,0:T(8,128)S(1)} %get-tuple-element.14.c, f32[2,32,8,256]{3,2,1,0:T(8,128)S(1)} %get-tuple-element.15.d), custom_call_target="tpu_custom_call" | custom-call | tf_op jit(solution)/shard_map/finish/pallas_call | solution.py:595
